TPU v7x, 32 devices: a whole 2x2x4 slice. The times are simulated.
32 devices in a mesh: leaf: 4 (over x, core), fsdp: 8 (over z, y).
Axes of the slice: x: 2, y: 2, z: 4, core: 2. Of those that a mesh axis runs over, the one named last changes fastest.
Arguments:
- layer_entry_matrix: bfloat16 [2, 8, 2048, 768], P(None, 'fsdp', 'leaf'), may hold values from -6 to 6
- loss_sensitivity: bfloat16 [2, 8, 2048, 768], P(None, 'fsdp', 'leaf'), may hold values from -6 to 6
- ancestor_block_table: int32 [2, 8, 16], P(None, 'fsdp'), may hold values from 0 to 15, as said below
- gate_trained_scores: float32 [12, 512, 512], P(None, 'fsdp'), may hold values from -6 to 6
- gate_random_jitter: float32 [12, 512, 512], P(None, 'fsdp'), may hold values from -6 to 6
- softening_scale: float32 [12], replicated, may hold values from 0.5 to 2
- triple_projection_matrix: bfloat16 [768, 2304], P('fsdp'), may hold values from -0.21875 to 0.21875
- asker_constant_vector: bfloat16 [768], P('fsdp'), may hold values from -3 to 3
- content_constant_vector: bfloat16 [768], P('fsdp'), may hold values from -3 to 3
- mixer_exit_matrix: bfloat16 [768, 768], P('fsdp'), may hold values from -9.75 to 9.75
- mixer_exit_constant: bfloat16 [768], P('fsdp'), may hold values from -3 to 3
- mixer_scaling_factor: bfloat16 [768], P('fsdp'), may hold values from 0.5 to 1.5
- mixer_recentering_term: bfloat16 [768], P('fsdp'), may hold values from -3 to 3
- dense_expand_matrix: bfloat16 [768, 3072], P('fsdp'), may hold values from -0.21875 to 0.21875
- dense_expand_constant: bfloat16 [3072], P('fsdp'), may hold values from -3 to 3
- dense_contract_matrix: bfloat16 [3072, 768], P('fsdp'), may hold values from -0.109375 to 0.109375
- dense_contract_constant: bfloat16 [768], P('fsdp'), may hold values from -3 to 3
- dense_scaling_factor: bfloat16 [768], P('fsdp'), may hold values from 0.5 to 1.5
- dense_recentering_term: bfloat16 [768], P('fsdp'), may hold values from -3 to 3
Outputs:
- layer_out: bfloat16 [2, 8, 2048, 768], P(None, 'fsdp', 'leaf')
- tokens_grad: bfloat16 [2, 8, 2048, 768], P(None, 'fsdp', 'leaf')
- qkv_weight_grad: float32 [768, 2304], P('fsdp')
- query_bias_grad: float32 [768], P('fsdp')
- value_bias_grad: float32 [768], P('fsdp')
- out_weight_grad: float32 [768, 768], P('fsdp')
- out_bias_grad: float32 [768], P('fsdp')
- first_gain_grad: float32 [768], P('fsdp')
- first_shift_grad: float32 [768], P('fsdp')
- up_weight_grad: float32 [768, 3072], P('fsdp')
- up_bias_grad: float32 [3072], P('fsdp')
- down_weight_grad: float32 [3072, 768], P('fsdp')
- down_bias_grad: float32 [768], P('fsdp')
- second_gain_grad: float32 [768], P('fsdp')
- second_shift_grad: float32 [768], P('fsdp')
- mask_logits_grad: float32 [12, 512, 512], P(None, 'fsdp')
Inputs may be any that keep to these rules, and one draw needn't show every extreme that they name: `ancestor_block_table`: in every tree, 4 trunk blocks form a chain whose first block is its own parent, 4 branch blocks have the last trunk block as parent, and 2 leaf blocks have each branch block as parent; the blocks stand in any order.
All inputs are finite; a program needn't handle non-finite values.
Results may differ from a plain program's by a relative error of at most 0.018.
Values may be sent and summed in bfloat16 or wider, within the bound.
A program may use at most 256 MiB of HBM per device.

v0:
```python
import math

import jax
import jax.numpy as jnp
from jax import lax
from jax.sharding import PartitionSpec as P

EPSILON = 1e-05
MASKED = -1e30
HIGHEST = lax.Precision.HIGHEST


def tree_tables(block_parent):
    blocks = block_parent.shape[0]
    indices = jnp.arange(blocks, dtype=jnp.int32)
    itself = (indices[:, None] == indices[None, :]).astype(jnp.int32)
    upward = (block_parent[:, None] == indices[None, :]).astype(jnp.int32)
    reachable = jnp.maximum(itself, upward)
    for rounds in range(blocks.bit_length()):
        reachable = jnp.minimum(jnp.dot(reachable, reachable), 1)
    depth_of = jnp.sum(reachable, axis=1, dtype=jnp.int32) - 1
    allowed = jnp.maximum(reachable, reachable.T) > 0
    return (depth_of, allowed)


def tree_layout(block_parent, leaf_index, row_count, leaf_count, mask_span):
    blocks = block_parent.shape[0]
    block_rows = row_count * leaf_count // blocks
    local_blocks = row_count // block_rows
    tile_count = mask_span // block_rows
    depth_of, allowed = tree_tables(block_parent)
    first_block = leaf_index * local_blocks
    local_depth = lax.dynamic_slice_in_dim(depth_of, first_block, local_blocks, 0)
    local_allowed = lax.dynamic_slice_in_dim(allowed, first_block, local_blocks, 0)
    tile_ids = jnp.arange(tile_count, dtype=jnp.int32)
    query_tiles = ((local_depth % tile_count)[:, None] == tile_ids[None, :]).astype(jnp.float32)
    key_tiles = ((depth_of % tile_count)[:, None] == tile_ids[None, :]).astype(jnp.float32)
    return (query_tiles, key_tiles, local_allowed)


def layer_norm(values, gain_vec, shift_vec):
    average = jnp.mean(values, axis=-1, keepdims=True)
    centred = values - average
    inv_scale = lax.rsqrt(jnp.mean(centred * centred, axis=-1, keepdims=True) + EPSILON)
    normed = centred * inv_scale
    return (normed * gain_vec + shift_vec, normed, inv_scale)


def norm_backward(upstream, normed, inv_scale, gain_vec):
    scaled = upstream * gain_vec
    inner_term = (
        scaled
        - jnp.mean(scaled, axis=-1, keepdims=True)
        - normed * jnp.mean(scaled * normed, axis=-1, keepdims=True)
    )
    return (inv_scale * inner_term, jnp.sum(upstream * normed, axis=0), jnp.sum(upstream, axis=0))


def gelu_slope(values):
    return 0.5 * (1.0 + lax.erf(values / math.sqrt(2.0))) + values * jnp.exp(
        -0.5 * values * values
    ) / math.sqrt(2.0 * math.pi)


def inner(left, right):
    return lax.dot_general(
        left, right, (((0,), (0,)), ((), ())), preferred_element_type=jnp.float32
    )


def dot_back(upstream, weight):
    return lax.dot_general(
        upstream, weight, (((1,), (1,)), ((), ())), preferred_element_type=jnp.float32
    )


def split_heads(matrix, head_count):
    return matrix.reshape(matrix.shape[0], head_count, matrix.shape[1] // head_count).transpose(
        1, 0, 2
    )


def merge_heads(tensor):
    return tensor.transpose(1, 0, 2).reshape(tensor.shape[1], tensor.shape[0] * tensor.shape[2])


def head_scores(query_head, key_head, mask_head, layout):
    query_tiles, key_tiles, local_allowed = layout
    local_blocks, tile_count = query_tiles.shape
    blocks = key_tiles.shape[0]
    row_count, head_size = query_head.shape
    block_rows = row_count // local_blocks
    score_scale = 1.0 / math.sqrt(head_size)
    raw_scores = (
        lax.dot_general(
            query_head, key_head, (((1,), (1,)), ((), ())), preferred_element_type=jnp.float32
        )
        * score_scale
    )
    raw_scores = raw_scores.reshape(local_blocks, block_rows, blocks, block_rows)
    scores = jnp.where(local_allowed[:, None, :, None], raw_scores, MASKED)
    mask_grid = mask_head.astype(jnp.float32).reshape(
        tile_count, block_rows, tile_count, block_rows
    )
    pair_mask = jnp.einsum("ai,ixjy,bj->axby", query_tiles, mask_grid, key_tiles, precision=HIGHEST)
    return (scores, pair_mask)


def attend_tree(query_tree, key_tree, value_tree, relaxed_mask, layout):
    head_count = relaxed_mask.shape[0]
    row_count = query_tree.shape[0]

    def one_head(pieces):
        query_head, key_head, value_head, mask_head = pieces
        scores, pair_mask = head_scores(query_head, key_head, mask_head, layout)
        row_max = jnp.max(scores, axis=(2, 3), keepdims=True)
        row_total = jnp.sum(jnp.exp(scores - row_max), axis=(2, 3), keepdims=True)
        log_total = row_max + jnp.log(row_total)
        weights = (
            (jnp.exp(scores - log_total) * pair_mask).astype(jnp.bfloat16).reshape(row_count, -1)
        )
        head_out = jnp.dot(weights, value_head, preferred_element_type=jnp.float32).astype(
            jnp.bfloat16
        )
        return (head_out, log_total.reshape(row_count))

    head_outs, log_totals = lax.map(
        one_head,
        (
            split_heads(query_tree, head_count),
            split_heads(key_tree, head_count),
            split_heads(value_tree, head_count),
            relaxed_mask,
        ),
    )
    return (merge_heads(head_outs), log_totals)


def head_backward(pieces, layout):
    query_head, key_head, value_head, mask_head, log_total, delta_head = pieces
    scores, pair_mask = head_scores(query_head, key_head, mask_head, layout)
    row_count, head_size = query_head.shape
    score_scale = 1.0 / math.sqrt(head_size)
    normalized = jnp.exp(scores - log_total.reshape(scores.shape[0], scores.shape[1], 1, 1))
    delta_weights = dot_back(delta_head, value_head).reshape(normalized.shape)
    delta_norm = delta_weights * pair_mask
    delta_pair = delta_weights * normalized
    row_term = jnp.sum(delta_norm * normalized, axis=(2, 3), keepdims=True)
    delta_scores = (
        (normalized * (delta_norm - row_term)).astype(jnp.bfloat16).reshape(row_count, -1)
    )
    delta_query = jnp.dot(delta_scores, key_head, preferred_element_type=jnp.float32) * score_scale
    query_tiles, key_tiles, local_allowed = layout
    delta_grid = jnp.einsum(
        "ai,axby,bj->ixjy", query_tiles, delta_pair, key_tiles, precision=HIGHEST
    )
    mask_span = mask_head.shape[0]
    delta_grid = delta_grid.reshape(mask_span, mask_span)
    weights = (normalized * pair_mask).astype(jnp.bfloat16).reshape(row_count, -1)
    delta_value = inner(weights, delta_head)
    delta_key = inner(delta_scores, query_head) * score_scale
    return (delta_query, delta_key, delta_value, delta_grid)


def forward_pass(block_tokens, layouts, params):
    (
        triple_projection_matrix,
        asker_constant_vector,
        content_constant_vector,
        mixer_exit_matrix,
        mixer_exit_constant,
        mixer_scaling_factor,
        mixer_recentering_term,
        dense_expand_matrix,
        dense_expand_constant,
        dense_contract_matrix,
        dense_contract_constant,
        dense_scaling_factor,
        dense_recentering_term,
        relaxed_mask,
    ) = params
    groups, row_count, model_width = block_tokens.shape
    flat_rows = block_tokens.reshape(groups * row_count, model_width)
    joined_proj = jnp.dot(flat_rows, triple_projection_matrix, preferred_element_type=jnp.float32)
    query_low = (joined_proj[:, :model_width] + asker_constant_vector.astype(jnp.float32)).astype(
        jnp.bfloat16
    )
    key_low = joined_proj[:, model_width : 2 * model_width].astype(jnp.bfloat16)
    value_low = (
        joined_proj[:, 2 * model_width :] + content_constant_vector.astype(jnp.float32)
    ).astype(jnp.bfloat16)
    own_keys = key_low.reshape(groups, row_count, model_width)
    own_values = value_low.reshape(groups, row_count, model_width)
    tree_keys, tree_values = (
        lax.all_gather(own_keys, "leaf", axis=1, tiled=True),
        lax.all_gather(own_values, "leaf", axis=1, tiled=True),
    )
    query_trees = query_low.reshape(groups, row_count, model_width)
    attended, log_totals = attend_tree(
        query_trees[0], tree_keys[0], tree_values[0], relaxed_mask, layouts[0]
    )
    log_parts = [log_totals]
    first_sum = (
        flat_rows.astype(jnp.float32)
        + jnp.dot(attended, mixer_exit_matrix, preferred_element_type=jnp.float32)
        + mixer_exit_constant.astype(jnp.float32)
    )
    hidden, normed_first, inv_first = layer_norm(
        first_sum,
        mixer_scaling_factor.astype(jnp.float32),
        mixer_recentering_term.astype(jnp.float32),
    )
    hidden_low = hidden.astype(jnp.bfloat16)
    up_proj = jnp.dot(
        hidden_low, dense_expand_matrix, preferred_element_type=jnp.float32
    ) + dense_expand_constant.astype(jnp.float32)
    active_low = jax.nn.gelu(up_proj, approximate=False).astype(jnp.bfloat16)
    second_sum = (
        hidden
        + jnp.dot(active_low, dense_contract_matrix, preferred_element_type=jnp.float32)
        + dense_contract_constant.astype(jnp.float32)
    )
    output, normed_second, inv_second = layer_norm(
        second_sum,
        dense_scaling_factor.astype(jnp.float32),
        dense_recentering_term.astype(jnp.float32),
    )
    saved = (
        flat_rows,
        query_trees,
        tree_keys,
        tree_values,
        log_parts,
        attended,
        normed_first,
        inv_first,
        hidden_low,
        up_proj,
        active_low,
        normed_second,
        inv_second,
        own_keys,
        own_values,
    )
    return (output.astype(jnp.bfloat16).reshape(groups, row_count, model_width), saved)


def backward_pass(block_cotangent, layouts, params, saved):
    (
        triple_projection_matrix,
        asker_constant_vector,
        content_constant_vector,
        mixer_exit_matrix,
        mixer_exit_constant,
        mixer_scaling_factor,
        mixer_recentering_term,
        dense_expand_matrix,
        dense_expand_constant,
        dense_contract_matrix,
        dense_contract_constant,
        dense_scaling_factor,
        dense_recentering_term,
        relaxed_mask,
    ) = params
    (
        flat_rows,
        query_trees,
        tree_keys,
        tree_values,
        log_parts,
        attended_low,
        normed_first,
        inv_first,
        hidden_low,
        up_proj,
        active_low,
        normed_second,
        inv_second,
        own_keys,
        own_values,
    ) = saved
    groups, row_count, model_width = block_cotangent.shape
    head_count = relaxed_mask.shape[0]
    delta_out = block_cotangent.reshape(groups * row_count, model_width).astype(jnp.float32)
    delta_second, second_gain_grad, second_shift_grad = norm_backward(
        delta_out, normed_second, inv_second, dense_scaling_factor.astype(jnp.float32)
    )
    delta_branch = delta_second.astype(jnp.bfloat16)
    down_weight_grad = inner(active_low, delta_branch)
    down_bias_grad = jnp.sum(delta_branch.astype(jnp.float32), axis=0)
    delta_active = dot_back(delta_branch, dense_contract_matrix)
    delta_up = (delta_active * gelu_slope(up_proj)).astype(jnp.bfloat16)
    up_weight_grad = inner(hidden_low, delta_up)
    up_bias_grad = jnp.sum(delta_up.astype(jnp.float32), axis=0)
    delta_hidden = delta_second + dot_back(delta_up, dense_expand_matrix)
    delta_first, first_gain_grad, first_shift_grad = norm_backward(
        delta_hidden, normed_first, inv_first, mixer_scaling_factor.astype(jnp.float32)
    )
    delta_proj = delta_first.astype(jnp.bfloat16)
    out_weight_grad = inner(attended_low, delta_proj)
    out_bias_grad = jnp.sum(delta_proj.astype(jnp.float32), axis=0)
    delta_attended = (
        dot_back(delta_proj, mixer_exit_matrix)
        .astype(jnp.bfloat16)
        .reshape(groups, row_count, model_width)
    )
    layout = layouts[0]
    delta_query, delta_key, delta_value, delta_grid = lax.map(
        lambda pieces: head_backward(pieces, layout),
        (
            split_heads(query_trees[0], head_count),
            split_heads(tree_keys[0], head_count),
            split_heads(tree_values[0], head_count),
            relaxed_mask,
            log_parts[0],
            split_heads(delta_attended[0], head_count),
        ),
    )
    query_parts = merge_heads(delta_query).astype(jnp.bfloat16)
    key_parts = [merge_heads(delta_key)]
    value_parts = [merge_heads(delta_value)]
    summed_keys, summed_values = (
        lax.psum_scatter(
            jnp.stack(key_parts).astype(jnp.bfloat16), "leaf", scatter_dimension=1, tiled=True
        ).astype(jnp.float32),
        lax.psum_scatter(
            jnp.stack(value_parts).astype(jnp.bfloat16), "leaf", scatter_dimension=1, tiled=True
        ).astype(jnp.float32),
    )
    key_grad_low = summed_keys.astype(jnp.bfloat16).reshape(groups * row_count, model_width)
    value_grad_low = summed_values.astype(jnp.bfloat16).reshape(groups * row_count, model_width)
    delta_joined = jnp.concatenate([query_parts, key_grad_low, value_grad_low], axis=1)
    qkv_weight_grad = inner(flat_rows, delta_joined)
    query_bias_grad = jnp.sum(query_parts.astype(jnp.float32), axis=0)
    value_bias_grad = jnp.sum(value_grad_low.astype(jnp.float32), axis=0)
    delta_tokens = (
        (delta_first + dot_back(delta_joined, triple_projection_matrix))
        .astype(jnp.bfloat16)
        .reshape(groups, row_count, model_width)
    )
    grads = (
        qkv_weight_grad,
        query_bias_grad,
        value_bias_grad,
        out_weight_grad,
        out_bias_grad,
        first_gain_grad,
        first_shift_grad,
        up_weight_grad,
        up_bias_grad,
        down_weight_grad,
        down_bias_grad,
        second_gain_grad,
        second_shift_grad,
        delta_grid,
    )
    return (delta_tokens, grads)


def per_device(
    layer_entry_matrix,
    loss_sensitivity,
    ancestor_block_table,
    gate_trained_scores,
    gate_random_jitter,
    softening_scale,
    triple_projection_matrix,
    asker_constant_vector,
    content_constant_vector,
    mixer_exit_matrix,
    mixer_exit_constant,
    mixer_scaling_factor,
    mixer_recentering_term,
    dense_expand_matrix,
    dense_expand_constant,
    dense_contract_matrix,
    dense_contract_constant,
    dense_scaling_factor,
    dense_recentering_term,
):
    micro_count, groups, row_count, model_width = layer_entry_matrix.shape
    leaf_count = lax.axis_size("leaf")
    leaf_index = lax.axis_index("leaf")
    mask_span = gate_trained_scores.shape[2]
    softened_entries = jax.nn.sigmoid(
        (gate_trained_scores + gate_random_jitter) / softening_scale[:, None, None]
    )
    relaxed_low = softened_entries.astype(jnp.bfloat16)
    out_parts = []
    delta_parts = []
    cumulative_sums = ()
    for batch_index in range(micro_count):
        layouts = [
            tree_layout(
                ancestor_block_table[batch_index, 0], leaf_index, row_count, leaf_count, mask_span
            )
        ]
        forward_set = (
            lax.all_gather(triple_projection_matrix, "fsdp", axis=0, tiled=True),
            lax.all_gather(asker_constant_vector, "fsdp", axis=0, tiled=True),
            lax.all_gather(content_constant_vector, "fsdp", axis=0, tiled=True),
            lax.all_gather(mixer_exit_matrix, "fsdp", axis=0, tiled=True),
            lax.all_gather(mixer_exit_constant, "fsdp", axis=0, tiled=True),
            lax.all_gather(mixer_scaling_factor, "fsdp", axis=0, tiled=True),
            lax.all_gather(mixer_recentering_term, "fsdp", axis=0, tiled=True),
            lax.all_gather(dense_expand_matrix, "fsdp", axis=0, tiled=True),
            lax.all_gather(dense_expand_constant, "fsdp", axis=0, tiled=True),
            lax.all_gather(dense_contract_matrix, "fsdp", axis=0, tiled=True),
            lax.all_gather(dense_contract_constant, "fsdp", axis=0, tiled=True),
            lax.all_gather(dense_scaling_factor, "fsdp", axis=0, tiled=True),
            lax.all_gather(dense_recentering_term, "fsdp", axis=0, tiled=True),
            lax.all_gather(relaxed_low, "fsdp", axis=1, tiled=True),
        )
        layer_rows, saved = forward_pass(layer_entry_matrix[batch_index], layouts, forward_set)
        backward_set = (
            lax.all_gather(triple_projection_matrix, "fsdp", axis=0, tiled=True),
            lax.all_gather(asker_constant_vector, "fsdp", axis=0, tiled=True),
            lax.all_gather(content_constant_vector, "fsdp", axis=0, tiled=True),
            lax.all_gather(mixer_exit_matrix, "fsdp", axis=0, tiled=True),
            lax.all_gather(mixer_exit_constant, "fsdp", axis=0, tiled=True),
            lax.all_gather(mixer_scaling_factor, "fsdp", axis=0, tiled=True),
            lax.all_gather(mixer_recentering_term, "fsdp", axis=0, tiled=True),
            lax.all_gather(dense_expand_matrix, "fsdp", axis=0, tiled=True),
            lax.all_gather(dense_expand_constant, "fsdp", axis=0, tiled=True),
            lax.all_gather(dense_contract_matrix, "fsdp", axis=0, tiled=True),
            lax.all_gather(dense_contract_constant, "fsdp", axis=0, tiled=True),
            lax.all_gather(dense_scaling_factor, "fsdp", axis=0, tiled=True),
            lax.all_gather(dense_recentering_term, "fsdp", axis=0, tiled=True),
            lax.all_gather(relaxed_low, "fsdp", axis=1, tiled=True),
        )
        delta_rows, grads = backward_pass(
            loss_sensitivity[batch_index], layouts, backward_set, saved
        )
        out_parts.append(layer_rows)
        delta_parts.append(delta_rows)
        if batch_index == 0:
            cumulative_sums = tuple(grads)
        else:
            cumulative_sums = tuple(jax.tree.map(jnp.add, tuple(cumulative_sums), tuple(grads)))
    cumulative_sums = (
        lax.psum_scatter(cumulative_sums[0], "fsdp", scatter_dimension=0, tiled=True),
        lax.psum_scatter(cumulative_sums[1], "fsdp", scatter_dimension=0, tiled=True),
        lax.psum_scatter(cumulative_sums[2], "fsdp", scatter_dimension=0, tiled=True),
        lax.psum_scatter(cumulative_sums[3], "fsdp", scatter_dimension=0, tiled=True),
        lax.psum_scatter(cumulative_sums[4], "fsdp", scatter_dimension=0, tiled=True),
        lax.psum_scatter(cumulative_sums[5], "fsdp", scatter_dimension=0, tiled=True),
        lax.psum_scatter(cumulative_sums[6], "fsdp", scatter_dimension=0, tiled=True),
        lax.psum_scatter(cumulative_sums[7], "fsdp", scatter_dimension=0, tiled=True),
        lax.psum_scatter(cumulative_sums[8], "fsdp", scatter_dimension=0, tiled=True),
        lax.psum_scatter(cumulative_sums[9], "fsdp", scatter_dimension=0, tiled=True),
        lax.psum_scatter(cumulative_sums[10], "fsdp", scatter_dimension=0, tiled=True),
        lax.psum_scatter(cumulative_sums[11], "fsdp", scatter_dimension=0, tiled=True),
        lax.psum_scatter(cumulative_sums[12], "fsdp", scatter_dimension=0, tiled=True),
        lax.psum_scatter(cumulative_sums[13], "fsdp", scatter_dimension=1, tiled=True),
    )
    cumulative_sums = (
        lax.psum(cumulative_sums[0].astype(jnp.bfloat16), "leaf").astype(jnp.float32),
        lax.psum(cumulative_sums[1].astype(jnp.bfloat16), "leaf").astype(jnp.float32),
        lax.psum(cumulative_sums[2].astype(jnp.bfloat16), "leaf").astype(jnp.float32),
        lax.psum(cumulative_sums[3].astype(jnp.bfloat16), "leaf").astype(jnp.float32),
        lax.psum(cumulative_sums[4].astype(jnp.bfloat16), "leaf").astype(jnp.float32),
        lax.psum(cumulative_sums[5].astype(jnp.bfloat16), "leaf").astype(jnp.float32),
        lax.psum(cumulative_sums[6].astype(jnp.bfloat16), "leaf").astype(jnp.float32),
        lax.psum(cumulative_sums[7].astype(jnp.bfloat16), "leaf").astype(jnp.float32),
        lax.psum(cumulative_sums[8].astype(jnp.bfloat16), "leaf").astype(jnp.float32),
        lax.psum(cumulative_sums[9].astype(jnp.bfloat16), "leaf").astype(jnp.float32),
        lax.psum(cumulative_sums[10].astype(jnp.bfloat16), "leaf").astype(jnp.float32),
        lax.psum(cumulative_sums[11].astype(jnp.bfloat16), "leaf").astype(jnp.float32),
        lax.psum(cumulative_sums[12].astype(jnp.bfloat16), "leaf").astype(jnp.float32),
        lax.psum(cumulative_sums[13].astype(jnp.bfloat16), "leaf").astype(jnp.float32),
    )
    mask_gradient = (
        cumulative_sums[13]
        * softened_entries
        * (1.0 - softened_entries)
        / softening_scale[:, None, None]
    )
    return (
        jnp.stack(out_parts),
        jnp.stack(delta_parts),
        cumulative_sums[0],
        cumulative_sums[1],
        cumulative_sums[2],
        cumulative_sums[3],
        cumulative_sums[4],
        cumulative_sums[5],
        cumulative_sums[6],
        cumulative_sums[7],
        cumulative_sums[8],
        cumulative_sums[9],
        cumulative_sums[10],
        cumulative_sums[11],
        cumulative_sums[12],
        mask_gradient,
    )


def solution(mesh):
    placed = (
        P(None, "fsdp", "leaf", None),
        P(None, "fsdp", "leaf", None),
        P(None, "fsdp", None),
        P(None, "fsdp", None),
        P(None, "fsdp", None),
        P(),
        P("fsdp", None),
        P("fsdp"),
        P("fsdp"),
        P("fsdp", None),
        P("fsdp"),
        P("fsdp"),
        P("fsdp"),
        P("fsdp", None),
        P("fsdp"),
        P("fsdp", None),
        P("fsdp"),
        P("fsdp"),
        P("fsdp"),
    )
    return jax.shard_map(
        per_device,
        mesh=mesh,
        in_specs=placed,
        out_specs=(
            P(None, "fsdp", "leaf", None),
            P(None, "fsdp", "leaf", None),
            P("fsdp", None),
            P("fsdp"),
            P("fsdp"),
            P("fsdp", None),
            P("fsdp"),
            P("fsdp"),
            P("fsdp"),
            P("fsdp", None),
            P("fsdp"),
            P("fsdp", None),
            P("fsdp"),
            P("fsdp"),
            P("fsdp"),
            P(None, "fsdp", None),
        ),
        check_vma=False,
    )
```

profile of v0, /device:TPU:0, one launch (start us, length us, event | category | flops | bytes accessed | tf_op | source)
XLA Modules:
  0.0 3312.0 jit_solution(5922466018517793214)
XLA Ops:
  8.0 70.1 %all-gather.15.cloned.1.call-done = bf16[768,2304]{1,0:T(8,128)(2,1)} async-done(((bf16[96,2304]{1,0:T(8,128)(2,1)}), bf16[768,2304]{1,0:T(8,128)(2,1)}) %all-gather.15.cloned.1.call-update) | async-done | bytes 3538960 | tf_op jit(solution)/shard_map/all_gather | solution.py:399
  96.1 34.6 %all-reduce.18 = (bf16[768]{0:T(1024)(128)(2,1)S(1)}, bf16[768]{0:T(1024)(128)(2,1)S(1)}, bf16[768]{0:T(1024)(128)(2,1)S(1)}, bf16[768]{0:T(1024)(128)(2,1)S(1)}...) all-reduce(bf16[768]{0:T(1024)(128)(2,1)S(1)} %dynamic-update-slice, ...), channel_id=1, replica_groups=mesh['leaf'=4,'fsdp'=8] {'fsdp'}, use_global_device_ids=true, to_apply=%add | all-reduce | flops 6144 | bytes 24576
  142.7 25.9 all-gather.4
  196.5 7.5 all-gather.27.cloned.1.call-done
  208.7 97.0 %all-gather.17.cloned.1.call-done = bf16[12,512,512]{2,1,0:T(8,128)(2,1)} async-done(((bf16[12,64,512]{2,1,0:T(8,128)(2,1)}), bf16[12,512,512]{2,1,0:T(8,128)(2,1)}) %all-gather.17.cloned.1.call-update) | async-done | bytes 6291472 | tf_op jit(solution)/shard_map/all_gather | solution.py:412
  305.7 212.4 %while.61 = (s32[]{:T(128)}, bf16[12,512,64]{1,2,0:T(8,128)(2,1)S(1)}, f32[12,512]{1,0:T(8,128)S(1)}, pred[4,16]{1,0:T(4,128)(4,1)S(1)}, bf16[12,512,64]{2,1,0:T...) while((s32[]{:T(128)}, ...), condition=%wide.region_13.14_spmd.clone, body=%wide.region_10.13_spmd.clone.sunk | while | flops 342916768 | bytes 42426708 | solution.py:127
  521.3 212.3 %while.60 = (s32[]{:T(128)}, bf16[12,512,64]{1,2,0:T(8,128)(2,1)S(1)}, f32[12,512]{1,0:T(8,128)S(1)}, pred[4,16]{1,0:T(4,128)(4,1)S(1)}, bf16[12,512,64]{2,1,0:T...) while((s32[]{:T(128)}, ...), condition=%wide.region_4.5_spmd.clone, body=%wide.region_1.4_spmd.clone.sunk | while | flops 342916768 | bytes 42426708 | solution.py:127
  744.9 31.7 fusion.194
  776.7 6.6 fusion.310
  791.9 8.2 convert_reduce_fusion.1
  810.3 7.1 convert_reduce_fusion.7
  824.8 6.2 broadcast.419.clone.1
  831.0 774.5 %while.62 = (s32[]{:T(128)}, bf16[12,512,64]{1,2,0:T(8,128)(2,1)S(1)}, bf16[12,2048,64]{1,2,0:T(8,128)(2,1)}, bf16[12,2048,64]{1,2,0:T(8,128)(2,1)}, f32[12,512,...) while((s32[]{:T(128)}, ...), condition=%wide.region_24.25_spmd.clone, body=%wide.region_22.24_spmd.clone.sunk | while | flops 812809984 | bytes 146293232 | solution.py:308
  881.1 5.5 copy.459
  945.6 5.5 copy.459
  1010.1 5.5 copy.459
  1074.5 5.5 copy.459
  1139.1 5.5 copy.459
  1203.5 5.5 copy.459
  1268.0 5.5 copy.459
  1332.5 5.5 copy.459
  1397.1 5.5 copy.459
  1461.5 5.5 copy.459
  1526.0 5.5 copy.459
  1590.5 5.5 copy.459
  1617.2 6.3 broadcast.419.clone
  1623.5 782.9 %while.63 = (s32[]{:T(128)}, bf16[12,512,64]{1,2,0:T(8,128)(2,1)S(1)}, bf16[12,2048,64]{1,2,0:T(8,128)(2,1)}, bf16[12,2048,64]{1,2,0:T(8,128)(2,1)}, f32[12,512,...) while((s32[]{:T(128)}, ...), condition=%wide.region_33.34_spmd.clone, body=%wide.region_31.33_spmd.clone.sunk | while | flops 812809984 | bytes 146293232 | solution.py:308
  1649.1 5.7 multiply_reduce_fusion.15
  1675.7 5.4 copy.475
  1805.8 5.4 copy.475
  1870.9 5.4 copy.475
  1936.0 5.4 copy.475
  2001.0 5.4 copy.475
  2412.2 6.2 fusion.298
  2418.5 5.7 convolution_add_fusion.1
  2436.0 6.5 fusion.250
  2443.4 40.7 %reduce-scatter.16.cloned.1.call-done = bf16[1,512,768]{1,2,0:T(8,128)(2,1)} async-done(((bf16[1,2048,768]{1,2,0:T(8,128)(2,1)}), bf16[1,512,768]{1,2,0:T(8,128)(2,1)}) %reduce-scatter.16.cloned.1.call-update) | async-done | bytes 786448 | tf_op jit(solution)/shard_map/reduce_scatter | solution.py:323
  2484.1 8.6 add_bitcast_fusion
  2492.7 8.0 copy.234
  2500.8 14.6 add.441
  2521.8 34.9 %reduce-scatter.20.cloned.1.call-done = f32[96,768]{1,0:T(8,128)} async-done(((f32[768,768]{1,0:T(8,128)}), f32[96,768]{1,0:T(8,128)}) %reduce-scatter.20.cloned.1.call-update) | async-done | bytes 294928 | tf_op jit(solution)/shard_map/reduce_scatter | solution.py:444
  2558.7 37.6 %all-reduce.17 = (bf16[768]{0:T(1024)(128)(2,1)S(1)}, bf16[768]{0:T(1024)(128)(2,1)S(1)}, bf16[768]{0:T(1024)(128)(2,1)S(1)}, bf16[768]{0:T(1024)(128)(2,1)S(1)}...) all-reduce(f32[768]{0:T(1024)S(1)} %add.429, ...), channel_id=11, replica_groups=mesh['leaf'=4,'fsdp'=8] {'fsdp'}, use_global_device_ids=true, to_apply=%region_40.41.clone | all-reduce | flops 9216 | bytes 55296
  2596.9 6.3 all-reduce.19
  2607.9 114.8 %reduce-scatter.22.cloned.1.call-done = f32[96,3072]{1,0:T(8,128)} async-done(((f32[768,3072]{1,0:T(8,128)}), f32[96,3072]{1,0:T(8,128)}) %reduce-scatter.22.cloned.1.call-update) | async-done | bytes 1179664 | tf_op jit(solution)/shard_map/reduce_scatter | solution.py:448
  2724.8 163.9 %reduce-scatter.24.cloned.1.call-done = f32[384,768]{1,0:T(8,128)} async-done(((f32[3072,768]{1,0:T(8,128)}), f32[384,768]{1,0:T(8,128)}) %reduce-scatter.24.cloned.1.call-update) | async-done | bytes 1179664 | tf_op jit(solution)/shard_map/reduce_scatter | solution.py:450
  2890.9 129.6 %reduce-scatter.28.cloned.1.call-done = f32[96,2304]{1,0:T(8,128)} async-done(((f32[768,2304]{1,0:T(8,128)}), f32[96,2304]{1,0:T(8,128)}) %reduce-scatter.28.cloned.1.call-update) | async-done | bytes 884752
  3022.6 208.5 %reduce-scatter.26.cloned.1.call-done = f32[12,64,512]{2,1,0:T(8,128)} async-done(((f32[12,512,512]{2,1,0:T(8,128)}), f32[12,64,512]{2,1,0:T(8,128)}) %reduce-scatter.26.cloned.1.call-update) | async-done | bytes 1572880 | tf_op jit(solution)/shard_map/reduce_scatter | solution.py:454
  3241.7 54.8 %all-reduce.23.cloned.1.call-done = (bf16[96,2304]{0,1:T(8,128)(2,1)}, bf16[96,768]{1,0:T(8,128)(2,1)}, bf16[96,3072]{1,0:T(8,128)(2,1)}, bf16[384,768]{1,0:T(8,128)(2,1)}, bf16[12,64,512]{2,1,0:T(8,128)(2,1)}) async-done(((bf16[96,2304]{0,1:T(8,128)(2,1)}, bf16[96,768]{1,0:T(8,128)(2,1)}, bf16[96,3072]{1,0:T(8,128)(2,1)}, bf16[384,768]{1,0:T(8,128)(2,1)}, bf16[12,64,512]{2,1,0:T(8,128)(2,1)}), ...) | async-done | bytes 2555920 | tf_op jit(solution)/shard_map/psum | solution.py:457
  (1410 shorter events, 2048.3 us)
Async XLA Ops:
  7.2 70.9 %all-gather.15.cloned.1.call-start = ((), (), s32[]{:S(2)}) async-start(), calls=%async_computation.9 | async-start | bytes 3981312 | tf_op jit(solution)/shard_map/all_gather | solution.py:399
  7.9 77.8 %copy-start.37 = (bf16[2,1,512,768]{3,2,1,0:T(8,128)(2,1)S(1)}, bf16[2,1,512,768]{3,2,1,0:T(8,128)(2,1)}, u32[]{:S(2)}) copy-start(bf16[2,1,512,768]{3,2,1,0:T(8,128)(2,1)} %param.27) | copy-start | bytes 4718596
  7.9 168.3 %all-gather.29.cloned.1.call-start = ((), (), s32[]{:S(2)}) async-start(), calls=%async_computation.24 | async-start | bytes 3932160 | tf_op jit(solution)/shard_map/all_gather | solution.py:195
  85.5 8.7 copy-start.88
  85.5 8.9 copy-start.89
  85.5 9.1 copy-start.90
  85.6 9.3 copy-start.91
  85.6 9.6 copy-start.92
  85.6 9.8 copy-start.93
  85.6 10.0 copy-start.94
  85.6 10.2 copy-start.95
  85.6 98.4 %all-gather.25.cloned.1.call-start = ((), (), s32[]{:S(2)}) async-start(), calls=%async_computation.22 | async-start | bytes 3932160 | tf_op jit(solution)/shard_map/all_gather | solution.py:195
  92.9 98.9 %all-gather.31.cloned.1.call-start = ((), (), s32[]{:S(2)}) async-start(), calls=%async_computation.25 | async-start | bytes 3932160 | tf_op jit(solution)/shard_map/all_gather | solution.py:196
  135.3 68.6 %all-gather.27.cloned.1.call-start = ((), (), s32[]{:S(2)}) async-start(), calls=%async_computation.23 | async-start | bytes 3932160 | tf_op jit(solution)/shard_map/all_gather | solution.py:196
  135.9 32.7 copy-start.81
  135.9 169.7 %all-gather.17.cloned.1.call-start = ((), (), s32[]{:S(2)}) async-start(), calls=%async_computation.10 | async-start | bytes 7077888 | tf_op jit(solution)/shard_map/all_gather | solution.py:412
  139.8 378.4 %all-gather.19.cloned.1.call-start = ((), (), s32[]{:S(2)}) async-start(), calls=%async_computation.11 | async-start | bytes 1327104 | tf_op jit(solution)/shard_map/all_gather | solution.py:402
  140.6 596.8 %all-gather.21.cloned.1.call-start = ((), (), s32[]{:S(2)}) async-start(), calls=%async_computation.12 | async-start | bytes 5308416 | tf_op jit(solution)/shard_map/all_gather | solution.py:406
  141.3 635.3 %all-gather.23.cloned.1.call-start = ((), (), s32[]{:S(2)}) async-start(), calls=%async_computation.13 | async-start | bytes 5308416 | tf_op jit(solution)/shard_map/all_gather | solution.py:408
  142.0 2293.3 %reduce-scatter.14.cloned.1.call-start = ((), (), s32[]{:S(2)}) async-start(), calls=%async_computation.15 | async-start | bytes 3932160 | tf_op jit(solution)/shard_map/reduce_scatter | solution.py:326
  169.7 613.9 %copy-start.47 = (f32[768]{0:T(1024)}, f32[768]{0:T(1024)S(1)}, u32[]{:S(2)}) copy-start(f32[768]{0:T(1024)S(1)} %convert_element_type.403) | copy-start | bytes 9220
  169.8 640.5 %copy-start.40 = (f32[768]{0:T(1024)}, f32[768]{0:T(1024)S(1)}, u32[]{:S(2)}) copy-start(f32[768]{0:T(1024)S(1)} %convert_element_type.402) | copy-start | bytes 9220
  520.8 289.4 %copy-start.4 = (f32[512,768]{1,0:T(8,128)}, f32[512,768]{1,0:T(8,128)S(1)}, u32[]{:S(2)}) copy-start(f32[512,768]{1,0:T(8,128)S(1)} %get-tuple-element.813) | copy-start | bytes 4718596
  520.8 289.4 %copy-start.50 = (f32[512]{0:T(512)}, f32[512]{0:T(512)S(1)}, u32[]{:S(2)}) copy-start(f32[512]{0:T(512)S(1)} %broadcast_multiply_fusion.9) | copy-start | bytes 6148
  521.2 289.0 %copy-start.54 = (f32[512]{0:T(512)}, f32[512]{0:T(512)S(1)}, u32[]{:S(2)}) copy-start(f32[512]{0:T(512)S(1)} %add_rsqrt_fusion.1) | copy-start | bytes 6148
  733.6 8.7 copy-start.25
  737.4 72.9 %copy-start.65 = (f32[512]{0:T(512)}, f32[512]{0:T(512)S(1)}, u32[]{:S(2)}) copy-start(f32[512]{0:T(512)S(1)} %broadcast_multiply_fusion.11) | copy-start | bytes 6148
  742.6 67.7 %copy-start.76 = (f32[512]{0:T(512)}, f32[512]{0:T(512)S(1)}, u32[]{:S(2)}) copy-start(f32[512]{0:T(512)S(1)} %add_rsqrt_fusion.3) | copy-start | bytes 6148
  744.9 31.7 copy-start.72
  789.0 11.2 slice-start
  789.0 16.0 slice-start.2
  791.9 18.4 copy-start.11
  791.9 13.1 slice-start.3
  810.3 8.3 copy-start.85
  1605.6 829.8 %reduce-scatter.12.cloned.1.call-start = ((), (), s32[]{:S(2)}) async-start(), calls=%async_computation.14 | async-start | bytes 3932160 | tf_op jit(solution)/shard_map/reduce_scatter | solution.py:323
  1612.9 830.5 %reduce-scatter.18.cloned.1.call-start = ((), (), s32[]{:S(2)}) async-start(), calls=%async_computation.17 | async-start | bytes 3932160 | tf_op jit(solution)/shard_map/reduce_scatter | solution.py:326
  2406.4 77.7 %reduce-scatter.16.cloned.1.call-start = ((), (), s32[]{:S(2)}) async-start(), calls=%async_computation.16 | async-start | bytes 3932160 | tf_op jit(solution)/shard_map/reduce_scatter | solution.py:323
  2407.1 149.5 %reduce-scatter.20.cloned.1.call-start = ((), (), s32[]{:S(2)}) async-start(), calls=%async_computation.18 | async-start | bytes 2654208 | tf_op jit(solution)/shard_map/reduce_scatter | solution.py:444
  2412.1 310.6 %reduce-scatter.22.cloned.1.call-start = ((), (), s32[]{:S(2)}) async-start(), calls=%async_computation.19 | async-start | bytes 10616832 | tf_op jit(solution)/shard_map/reduce_scatter | solution.py:448
  2424.2 464.5 %reduce-scatter.24.cloned.1.call-start = ((), (), s32[]{:S(2)}) async-start(), calls=%async_computation.20 | async-start | bytes 10616832 | tf_op jit(solution)/shard_map/reduce_scatter | solution.py:450
  2434.9 585.6 %reduce-scatter.28.cloned.1.call-start = ((), (), s32[]{:S(2)}) async-start(), calls=%async_computation.26 | async-start | bytes 7962624
  2500.8 730.4 %reduce-scatter.26.cloned.1.call-start = ((), (), s32[]{:S(2)}) async-start(), calls=%async_computation.21 | async-start | bytes 14155776 | tf_op jit(solution)/shard_map/reduce_scatter | solution.py:454
  2515.5 781.0 %all-reduce.23.cloned.1.call-start = ((), (), s32[]{:S(2)}) async-start(), calls=%async_computation.27 | async-start | bytes 5406720 | tf_op jit(solution)/shard_map/psum | solution.py:457
  2517.2 41.1 %copy-start.33 = (bf16[1,512,768]{1,2,0:T(8,128)(2,1)S(1)}, bf16[1,512,768]{1,2,0:T(8,128)(2,1)}, u32[]{:S(2)}) copy-start(bf16[1,512,768]{1,2,0:T(8,128)(2,1)} %reduce-scatter.14.cloned.1.call-done) | copy-start | bytes 2359300
  2517.2 41.3 %copy-start.28 = (bf16[1,512,768]{1,2,0:T(8,128)(2,1)S(1)}, bf16[1,512,768]{1,2,0:T(8,128)(2,1)}, u32[]{:S(2)}) copy-start(bf16[1,512,768]{1,2,0:T(8,128)(2,1)} %reduce-scatter.18.cloned.1.call-done) | copy-start | bytes 2359300
  2890.9 342.7 %copy-start.16 = (f32[512,768]{1,0:T(8,128)S(1)}, f32[512,768]{1,0:T(8,128)}, u32[]{:S(2)}) copy-start(f32[512,768]{1,0:T(8,128)} %copy-done.14) | copy-start | bytes 4718596
  3241.7 62.1 %copy-start.17 = (f32[12,64,512]{2,1,0:T(8,128)S(1)}, f32[12,64,512]{2,1,0:T(8,128)}, u32[]{:S(2)}) copy-start(f32[12,64,512]{2,1,0:T(8,128)} %get-tuple-element.762) | copy-start | bytes 4718596
  3241.7 62.1 %copy-start.74 = (f32[12]{0:T(128)S(1)}, f32[12]{0:T(128)}, u32[]{:S(2)}) copy-start(f32[12]{0:T(128)} %param.32) | copy-start | bytes 148
  (117 other events, 552.9 us)
Sparse Core Ops, SparseCore 0:
  10.2 67.8 all-gather.14
  85.6 27.0 all-gather.28
  114.2 28.5 all-gather.24
  144.8 28.5 all-gather.30
  175.4 28.5 all-gather.26
  206.5 99.0 all-gather.16
  307.8 39.2 all-gather.18
  349.3 78.6 all-gather.20
  430.2 78.0 all-gather.22
  1605.7 37.1 reduce-scatter.13
  1645.6 37.9 reduce-scatter.11
  2406.5 36.8 reduce-scatter.17
  2446.1 37.9 reduce-scatter.15
  2487.4 69.1 reduce-scatter.19
  2560.1 162.5 reduce-scatter.21
  2726.1 162.5 reduce-scatter.23
  2892.2 128.1 reduce-scatter.27
  3024.3 206.7 reduce-scatter.25
  3235.2 61.2 all-reduce.22
where the time goes:
time: 3340 us; the launch traced here: 3310 us
  matrix products  1040 us (31%)
  local copies, waits for them, and re-layouts  998 us (30%)
  waiting for transfers between devices  927 us (28%)
  other arithmetic  223 us (7%)
  blocking collectives  104 us (3%)
    dot_general x96, matrix products, head_scores(): jnp.einsum('ai,ixjy,bj->axby', query_tiles, mask_grid, key_tiles, precisi...  274 us
    reduce_scatter x1, waiting for transfers between devices, per_device(): lax.psum_scatter(cumulative_sums[13], 'fsdp', scatter_dimension=1, tiled=...  209 us
    while x192, local copies, waits for them, and re-layouts  188 us
    dot_general x56, matrix products, inner(): lax.dot_general(left, right, (((0,), (0,)), ((), ())), preferred_element_...  179 us
    dot_general x48, matrix products, head_backward(): jnp.einsum('ai,axby,bj->ixjy', query_tiles, delta_pair, key_tiles, precis...  167 us
    reduce_scatter x1, waiting for transfers between devices, per_device(): lax.psum_scatter(cumulative_sums[9], 'fsdp', scatter_dimension=0, tiled=T...  164 us
    dot_general x32, matrix products, dot_back(): lax.dot_general(upstream, weight, (((1,), (1,)), ((), ())), preferred_ele...  157 us
    unnamed x20, waiting for transfers between devices  134 us
  transfers between devices with their start and end apart: 19, of which 11 were waited for; matrix products, arithmetic and copies ran while one was open for 42% of the time, Pallas kernels for 0%

commit v1 on v0

v1 whole, which is shorter than its diff:
```python
import functools
import math

import jax
import jax.numpy as jnp
from jax import lax
from jax.experimental import pallas as pl
from jax.experimental.pallas import tpu as pltpu
from jax.sharding import PartitionSpec as P

EPSILON = 1e-05
F32 = jnp.float32
BF = jnp.bfloat16
TRUNK = 4
GROUPS = 4
CORES = 2
LOW_HALF = 64


def layer_norm(values, gain_vec, shift_vec):
    average = jnp.mean(values, axis=-1, keepdims=True)
    centred = values - average
    inv_scale = lax.rsqrt(jnp.mean(centred * centred, axis=-1, keepdims=True) + EPSILON)
    normed = centred * inv_scale
    return (normed * gain_vec + shift_vec, normed, inv_scale)


def norm_backward(upstream, normed, inv_scale, gain_vec):
    scaled = upstream * gain_vec
    inner_term = (
        scaled
        - jnp.mean(scaled, axis=-1, keepdims=True)
        - normed * jnp.mean(scaled * normed, axis=-1, keepdims=True)
    )
    return (inv_scale * inner_term, jnp.sum(upstream * normed, axis=0), jnp.sum(upstream, axis=0))


def gelu_parts(values):
    cdf = 0.5 * (1.0 + lax.erf(values / math.sqrt(2.0)))
    density = jnp.exp(-0.5 * values * values) / math.sqrt(2.0 * math.pi)
    return (values * cdf, cdf + values * density)


def dot_nn(left, right):
    return jnp.dot(left, right, preferred_element_type=F32)


def dot_nt(left, right):
    return lax.dot_general(left, right, (((1,), (1,)), ((), ())), preferred_element_type=F32)


def dot_tn(left, right):
    return lax.dot_general(left, right, (((0,), (0,)), ((), ())), preferred_element_type=F32)


def tree_order(parent):
    count = parent.shape[0]
    ids = jnp.arange(count, dtype=jnp.int32)
    up = (parent[:, None] == ids[None, :]) & (ids[:, None] != ids[None, :])
    up = up.astype(F32)
    reach = up
    power = up
    for _ in range(TRUNK + 1):
        power = jnp.sum(power[:, :, None] * up[None, :, :], axis=1)
        reach = reach + power
    depth = jnp.sum(reach, axis=1)
    before = (ids[None, :] < ids[:, None]).astype(F32)
    branch = (depth == TRUNK).astype(F32)
    rank = jnp.sum(before * branch[None, :], axis=1)
    own_rank = jnp.where(depth == TRUNK, rank, jnp.sum(up * rank[None, :], axis=1))
    siblings = jnp.sum(up[:, None, :] * up[None, :, :], axis=2) * before
    second = jnp.sum(siblings, axis=1)
    within = jnp.where(depth == TRUNK, 1.0, 2.0 * second)
    place = jnp.where(depth < TRUNK, depth, TRUNK + 3.0 * own_rank + within).astype(jnp.int32)
    order = jnp.sum((place[:, None] == ids[None, :]) * ids[:, None], axis=0).astype(jnp.int32)
    return (order, place)


def low_lanes():
    return lax.broadcasted_iota(jnp.int32, (1, 2 * LOW_HALF), 1) < LOW_HALF


def one_head(pair, which):
    keep = low_lanes() if which == 0 else jnp.logical_not(low_lanes())
    return jnp.where(keep, pair, jnp.zeros_like(pair))


def group_columns(row, block):
    return ((0, 2 * block, (1, 0)), (0, 3 * block, (1, 0, 1)), (block, 2 * block, (0, 1)))[row]


def mask_columns(mask_rows, tiles, block):
    return jnp.concatenate([mask_rows[:, t * block : (t + 1) * block] for t in tiles], axis=1)


def attend_kernel(block, query_ref, key_ref, value_ref, mask_ref, out_ref, log_ref):
    trunk = TRUNK * block
    wide = 3 * block
    low = low_lanes()

    def soften(parts, masks, values):
        top = parts[0].max(axis=1, keepdims=True)
        for part in parts[1:]:
            top = jnp.maximum(top, part.max(axis=1, keepdims=True))
        total = 0.0
        out = 0.0
        for part, mask, value in zip(parts, masks, values):
            weight = jnp.exp(part - top)
            total = total + weight.sum(axis=1, keepdims=True)
            out = out + dot_nn((weight * mask.astype(F32)).astype(BF), value)
        return (out * (1.0 / total), top + jnp.log(total))

    def emit(rows, results):
        count = results[0][1].shape[0]
        out_ref[rows, :] = jnp.where(low, results[0][0], results[1][0]).astype(BF)
        logs = [jnp.broadcast_to(result[1], (count, 2 * LOW_HALF)) for result in results]
        log_ref[rows, :] = jnp.where(low, logs[0], logs[1])

    def trunk_rows(index, carry):
        rows = pl.ds(pl.multiple_of(index * block, block), block)
        query = query_ref[rows, :]
        results = []
        for which in range(2):
            mask_rows = mask_ref[which, rows, :]
            columns = [(0, trunk, mask_rows)]
            side = mask_columns(mask_rows, (1, 0, 1), block)
            columns += [(trunk + wide * g, wide, side) for g in range(GROUPS)]
            head = one_head(query, which)
            parts = [dot_nt(head, key_ref[c : c + w, :]) for c, w, _ in columns]
            values = [value_ref[c : c + w, :] for c, w, _ in columns]
            results.append(soften(parts, [column[2] for column in columns], values))
        emit(rows, results)
        return carry

    lax.fori_loop(0, TRUNK, trunk_rows, 0)

    def group_rows(group, carry):
        base = pl.multiple_of(trunk + wide * group, block)
        for row in range(3):
            rows = pl.ds(pl.multiple_of(base + block * row, block), block)
            query = query_ref[rows, :]
            tile = 0 if row == 1 else 1
            start, width, tiles = group_columns(row, block)
            columns = pl.ds(pl.multiple_of(base + start, block), width)
            results = []
            for which in range(2):
                mask_rows = mask_ref[which, tile * block : (tile + 1) * block, :]
                head = one_head(query, which)
                parts = [dot_nt(head, key_ref[0:trunk, :]), dot_nt(head, key_ref[columns, :])]
                masks = [mask_rows, mask_columns(mask_rows, tiles, block)]
                values = [value_ref[0:trunk, :], value_ref[columns, :]]
                results.append(soften(parts, masks, values))
            emit(rows, results)
        return carry

    lax.fori_loop(0, GROUPS, group_rows, 0)


def attend(query, key, value, mask, block):
    rows, width = query.shape
    pairs = width // (2 * LOW_HALF)
    span = mask.shape[1]
    spec = pl.BlockSpec((rows, 2 * LOW_HALF), lambda p: (0, p))
    return pl.pallas_call(
        functools.partial(attend_kernel, block),
        grid=(pairs,),
        name="attend",
        in_specs=[spec, spec, spec, pl.BlockSpec((2, span, span), lambda p: (p, 0, 0))],
        out_specs=[spec, spec],
        out_shape=[
            jax.ShapeDtypeStruct((rows, width), BF),
            jax.ShapeDtypeStruct((rows, width), F32),
        ],
        compiler_params=pltpu.CompilerParams(vmem_limit_bytes=48 << 20),
    )(query, key, value, mask)


def attend_back_kernel(
    block,
    scale,
    query_ref,
    key_ref,
    value_ref,
    mask_ref,
    out_ref,
    log_ref,
    delta_ref,
    dquery_ref,
    dkey_ref,
    dvalue_ref,
    dmask_ref,
    key_sum,
    value_sum,
    query_turned,
    delta_turned,
):
    trunk = TRUNK * block
    wide = 3 * block
    low = low_lanes()
    key_sum[...] = jnp.zeros_like(key_sum)
    value_sum[...] = jnp.zeros_like(value_sum)
    dmask_ref[...] = jnp.zeros_like(dmask_ref)
    query_turned[...] = query_ref[...].astype(F32).T.astype(BF)
    delta_turned[...] = delta_ref[...].astype(F32).T.astype(BF)

    def work(rows, mask_place, columns):
        query = query_ref[rows, :]
        delta = delta_ref[rows, :]
        product = delta.astype(F32) * out_ref[rows, :].astype(F32)
        logs = log_ref[rows, :]
        dqueries = []
        for which in range(2):
            first = LOW_HALF * which
            lanes = slice(first, first + LOW_HALF)
            query_head = one_head(query, which)
            delta_head = one_head(delta, which)
            log = logs[:, first : first + 1]
            row_term = jnp.sum(product[:, lanes], axis=1, keepdims=True)
            mask_rows = mask_ref[which, mask_place, :]
            dquery = 0.0
            for place, tiles in columns:
                key = key_ref[place, :]
                value = value_ref[place, :]
                probs = jnp.exp(dot_nt(query_head, key) - log)
                pair = dot_nt(delta_head, value) * probs
                mask = mask_rows if tiles is None else mask_columns(mask_rows, tiles, block)
                mask = mask.astype(F32)
                if tiles is None:
                    dmask_ref[which, mask_place, :] += pair
                else:
                    for tile in sorted(set(tiles)):
                        dmask_ref[which, mask_place, tile * block : (tile + 1) * block] += sum(
                            pair[:, a * block : (a + 1) * block]
                            for a, t in enumerate(tiles)
                            if t == tile
                        )
                dscores = (pair * mask - probs * row_term).astype(BF)
                weights = (probs * mask).astype(BF)
                dquery = dquery + dot_nn(dscores, key)
                key_sum[lanes, place] += dot_nn(query_turned[lanes, rows], dscores)
                value_sum[lanes, place] += dot_nn(delta_turned[lanes, rows], weights)
            dqueries.append(dquery)
        dquery_ref[rows, :] = (jnp.where(low, dqueries[0], dqueries[1]) * scale).astype(BF)

    def trunk_rows(index, carry):
        rows = pl.ds(pl.multiple_of(index * block, block), block)
        columns = [(pl.ds(0, trunk), None)]
        columns += [(pl.ds(trunk + wide * g, wide), (1, 0, 1)) for g in range(GROUPS)]
        work(rows, rows, columns)
        return carry

    lax.fori_loop(0, TRUNK, trunk_rows, 0)

    def group_rows(group, carry):
        base = pl.multiple_of(trunk + wide * group, block)
        for row in range(3):
            rows = pl.ds(pl.multiple_of(base + block * row, block), block)
            tile = 0 if row == 1 else 1
            start, width, tiles = group_columns(row, block)
            near = pl.ds(pl.multiple_of(base + start, block), width)
            work(rows, pl.ds(tile * block, block), [(pl.ds(0, trunk), None), (near, tiles)])
        return carry

    lax.fori_loop(0, GROUPS, group_rows, 0)
    dkey_ref[...] = key_sum[...].T.astype(BF)
    dvalue_ref[...] = value_sum[...].T.astype(BF)


def attend_back(query, key, value, mask, out, logs, delta, block, scale):
    rows, width = query.shape
    pair_width = 2 * LOW_HALF
    pairs = width // pair_width
    span = mask.shape[1]
    spec = pl.BlockSpec((rows, pair_width), lambda p: (0, p))
    mask_spec = pl.BlockSpec((2, span, span), lambda p: (p, 0, 0))
    return pl.pallas_call(
        functools.partial(attend_back_kernel, block, scale),
        grid=(pairs,),
        name="attend_back",
        in_specs=[spec, spec, spec, mask_spec, spec, spec, spec],
        out_specs=[spec, spec, spec, mask_spec],
        out_shape=[jax.ShapeDtypeStruct((rows, width), BF)] * 3
        + [jax.ShapeDtypeStruct(mask.shape, F32)],
        scratch_shapes=[
            pltpu.VMEM((pair_width, rows), F32),
            pltpu.VMEM((pair_width, rows), F32),
            pltpu.VMEM((pair_width, rows), BF),
            pltpu.VMEM((pair_width, rows), BF),
        ],
        compiler_params=pltpu.CompilerParams(vmem_limit_bytes=48 << 20),
    )(query, key, value, mask, out, logs, delta)


def reorder_kernel(order_ref, source_ref, target_ref):
    target_ref[...] = source_ref[...]


def reorder(tokens, order):
    count, block, width = tokens.shape
    return pl.pallas_call(
        reorder_kernel,
        name="reorder",
        grid_spec=pltpu.PrefetchScalarGridSpec(
            num_scalar_prefetch=1,
            grid=(count,),
            in_specs=[pl.BlockSpec((1, block, width), lambda i, order_ref: (order_ref[i], 0, 0))],
            out_specs=pl.BlockSpec((1, block, width), lambda i, order_ref: (i, 0, 0)),
        ),
        out_shape=jax.ShapeDtypeStruct(tokens.shape, tokens.dtype),
    )(order, tokens)


def gather_rows(array, axis=0):
    return lax.all_gather(array, "fsdp", axis=axis, tiled=True)


def per_device(
    layer_entry_matrix,
    loss_sensitivity,
    ancestor_block_table,
    gate_trained_scores,
    gate_random_jitter,
    softening_scale,
    triple_projection_matrix,
    asker_constant_vector,
    content_constant_vector,
    mixer_exit_matrix,
    mixer_exit_constant,
    mixer_scaling_factor,
    mixer_recentering_term,
    dense_expand_matrix,
    dense_expand_constant,
    dense_contract_matrix,
    dense_contract_constant,
    dense_scaling_factor,
    dense_recentering_term,
):
    micro, _, own_rows, width = layer_entry_matrix.shape
    leaf_count = lax.axis_size("leaf")
    blocks = ancestor_block_table.shape[2]
    rows = own_rows * leaf_count
    block = rows // blocks
    heads, _, span = gate_trained_scores.shape
    leaf = lax.axis_index("leaf")
    tree = leaf // CORES
    core = leaf % CORES
    my_heads = heads // CORES
    my_width = width // CORES
    half = rows // CORES
    pairs = [[CORES * i + c for c in range(CORES)] for i in range(leaf_count // CORES)]
    score_scale = 1.0 / math.sqrt(width // heads)

    orders = [tree_order(ancestor_block_table[m, 0]) for m in range(micro)]
    order = jnp.where(tree == 0, orders[0][0], orders[1][0])

    def own_tree(tokens):
        whole = lax.all_gather(tokens[:, 0], "leaf", axis=1, tiled=True)
        mine = lax.dynamic_index_in_dim(whole, tree, 0, keepdims=False)
        return reorder(mine.reshape(blocks, block, width), order).reshape(rows, width)

    def own_tokens(halves):
        whole = lax.all_gather(halves, "leaf", axis=0, tiled=True)
        whole = whole.reshape(micro, blocks, block, width)
        mine = [reorder(whole[m], orders[m][1]) for m in range(micro)]
        mine = jnp.stack(mine).reshape(micro, 1, rows, width)
        return lax.dynamic_slice_in_dim(mine, leaf * own_rows, own_rows, 2)

    def own_half(array):
        return lax.dynamic_slice_in_dim(array, core * half, half, 0)

    softened = jax.nn.sigmoid(
        (gate_trained_scores + gate_random_jitter) / softening_scale[:, None, None]
    )
    relaxed = lax.dynamic_slice_in_dim(softened.astype(BF), core * my_heads, my_heads, 0)
    mask = gather_rows(relaxed, 1)
    joined_weight = gather_rows(triple_projection_matrix)
    out_weight = gather_rows(mixer_exit_matrix)
    up_weight = gather_rows(dense_expand_matrix)
    down_weight = gather_rows(dense_contract_matrix)
    vectors = [
        asker_constant_vector,
        content_constant_vector,
        mixer_exit_constant,
        mixer_scaling_factor,
        mixer_recentering_term,
        dense_contract_constant,
        dense_scaling_factor,
        dense_recentering_term,
        dense_expand_constant,
    ]
    packed = gather_rows(jnp.concatenate(vectors)[None])
    places = []
    first = 0
    for vector in vectors:
        places.append((first, first + vector.shape[0]))
        first += vector.shape[0]
    (
        query_bias,
        value_bias,
        out_bias,
        first_gain,
        first_shift,
        down_bias,
        second_gain,
        second_shift,
        up_bias,
    ) = [packed[:, a:b].reshape(-1).astype(F32) for a, b in places]

    tokens = own_tree(layer_entry_matrix)
    upstream = own_half(own_tree(loss_sensitivity)).astype(F32)

    def my_columns(matrix, which):
        return lax.dynamic_slice_in_dim(matrix, which * width + core * my_width, my_width, 1)

    def my_part(vector):
        return lax.dynamic_slice_in_dim(vector, core * my_width, my_width, 0)

    weight3 = jnp.concatenate([my_columns(joined_weight, i) for i in range(3)], axis=1)
    joined = dot_nn(tokens, weight3)
    query = (joined[:, :my_width] + my_part(query_bias)).astype(BF) * jnp.asarray(score_scale, BF)
    key = joined[:, my_width : 2 * my_width].astype(BF)
    value = (joined[:, 2 * my_width :] + my_part(value_bias)).astype(BF)

    attended_mine, logs = attend(query, key, value, mask, block)
    attended = own_half(
        lax.all_gather(attended_mine, "leaf", axis=1, tiled=True, axis_index_groups=pairs)
    )

    rows_mine = own_half(tokens).astype(F32)
    hidden, normed_first, inv_first = layer_norm(
        rows_mine + dot_nn(attended, out_weight) + out_bias, first_gain, first_shift
    )
    hidden_low = hidden.astype(BF)
    active, slope = gelu_parts(dot_nn(hidden_low, up_weight) + up_bias)
    active = active.astype(BF)
    output, normed_second, inv_second = layer_norm(
        hidden + dot_nn(active, down_weight) + down_bias, second_gain, second_shift
    )
    layer_out = own_tokens(output.astype(BF))

    delta_second, second_gain_grad, second_shift_grad = norm_backward(
        upstream, normed_second, inv_second, second_gain
    )
    delta_branch = delta_second.astype(BF)
    down_weight_grad = dot_tn(active, delta_branch)
    down_bias_grad = jnp.sum(delta_branch.astype(F32), axis=0)
    delta_up = (dot_nt(delta_branch, down_weight) * slope).astype(BF)
    up_weight_grad = dot_tn(hidden_low, delta_up)
    up_bias_grad = jnp.sum(delta_up.astype(F32), axis=0)
    delta_first, first_gain_grad, first_shift_grad = norm_backward(
        delta_second + dot_nt(delta_up, up_weight), normed_first, inv_first, first_gain
    )
    delta_proj = delta_first.astype(BF)
    out_weight_grad = dot_tn(attended, delta_proj)
    out_bias_grad = jnp.sum(delta_proj.astype(F32), axis=0)
    delta_attended = lax.all_gather(
        dot_nt(delta_proj, out_weight).astype(BF),
        "leaf",
        axis=0,
        tiled=True,
        axis_index_groups=pairs,
    )
    delta_attended = lax.dynamic_slice_in_dim(delta_attended, core * my_width, my_width, 1)

    dquery, dkey, dvalue, dmask = attend_back(
        query, key, value, mask, attended_mine, logs, delta_attended, block, score_scale
    )
    djoined = jnp.concatenate([dquery, dkey, dvalue], axis=1)
    joined_grad = dot_tn(tokens, djoined)
    query_bias_grad = jnp.sum(dquery.astype(F32), axis=0)
    value_bias_grad = jnp.sum(dvalue.astype(F32), axis=0)
    dtokens = lax.psum_scatter(
        dot_nt(djoined, weight3).astype(BF),
        "leaf",
        scatter_dimension=0,
        tiled=True,
        axis_index_groups=pairs,
    )
    tokens_grad = own_tokens((delta_first + dtokens.astype(F32)).astype(BF))

    def placed(part, whole_size, start, axis):
        shape = list(part.shape)
        shape[axis] = whole_size
        return lax.dynamic_update_slice_in_dim(jnp.zeros(shape, part.dtype), part, start, axis)

    def owned(grad, axis=0):
        return lax.psum_scatter(
            grad.astype(BF), "fsdp", scatter_dimension=axis, tiled=True
        )

    joined_part = owned(joined_grad)
    joined_full = jnp.zeros((joined_part.shape[0], 3 * width), BF)
    for i in range(3):
        joined_full = lax.dynamic_update_slice_in_dim(
            joined_full,
            joined_part[:, i * my_width : (i + 1) * my_width],
            i * width + core * my_width,
            1,
        )
    matrices = (
        joined_full,
        owned(out_weight_grad),
        owned(up_weight_grad),
        owned(down_weight_grad),
        placed(owned(dmask, 1), heads, core * my_heads, 0),
    )
    joined_total, out_total, up_total, down_total, mask_total = [
        lax.psum(matrix, "leaf").astype(F32) for matrix in matrices
    ]
    small = (
        placed(query_bias_grad, width, core * my_width, 0),
        placed(value_bias_grad, width, core * my_width, 0),
        out_bias_grad,
        first_gain_grad,
        first_shift_grad,
        up_bias_grad,
        down_bias_grad,
        second_gain_grad,
        second_shift_grad,
    )
    fsdp_count = lax.axis_size("fsdp")
    packed_grads = jnp.concatenate([s.reshape(fsdp_count, -1) for s in small], axis=1)
    packed_grads = lax.psum(
        lax.psum_scatter(packed_grads, "fsdp", scatter_dimension=0, tiled=True), "leaf"
    )[0]
    vector_grads = []
    first = 0
    for s in small:
        size = s.shape[0] // fsdp_count
        vector_grads.append(packed_grads[first : first + size])
        first += size
    mask_gradient = mask_total * softened * (1.0 - softened) / softening_scale[:, None, None]
    return (
        layer_out,
        tokens_grad,
        joined_total,
        vector_grads[0],
        vector_grads[1],
        out_total,
        vector_grads[2],
        vector_grads[3],
        vector_grads[4],
        up_total,
        vector_grads[5],
        down_total,
        vector_grads[6],
        vector_grads[7],
        vector_grads[8],
        mask_gradient,
    )


def solution(mesh):
    placed = (
        P(None, "fsdp", "leaf", None),
        P(None, "fsdp", "leaf", None),
        P(None, "fsdp", None),
        P(None, "fsdp", None),
        P(None, "fsdp", None),
        P(),
        P("fsdp", None),
        P("fsdp"),
        P("fsdp"),
        P("fsdp", None),
        P("fsdp"),
        P("fsdp"),
        P("fsdp"),
        P("fsdp", None),
        P("fsdp"),
        P("fsdp", None),
        P("fsdp"),
        P("fsdp"),
        P("fsdp"),
    )
    return jax.shard_map(
        per_device,
        mesh=mesh,
        in_specs=placed,
        out_specs=(
            P(None, "fsdp", "leaf", None),
            P(None, "fsdp", "leaf", None),
            P("fsdp", None),
            P("fsdp"),
            P("fsdp"),
            P("fsdp", None),
            P("fsdp"),
            P("fsdp"),
            P("fsdp"),
            P("fsdp", None),
            P("fsdp"),
            P("fsdp", None),
            P("fsdp"),
            P("fsdp"),
            P("fsdp"),
            P(None, "fsdp", None),
        ),
        check_vma=False,
    )
```

time: 3340 us -> 1240 us (0.37)
  matrix products: 1040 us -> 93.7 us
  local copies, waits for them, and re-layouts: 998 us -> 64.1 us
  Pallas kernels: 0 us -> 192 us
  other arithmetic: 223 us -> 33.6 us
  waiting for transfers between devices: 927 us -> 754 us
    dot_general x342 -> x12, matrix products: 1040 us -> 93.7 us  [the longest x4 33 us: dot_nn(): return jnp.dot(left, right, preferred_element_type=F32)]
    pallas_call x0 -> x8, Pallas kernels: none -> 192 us  [the longest x1 83.5 us: attend_back(): pl.pallas_call(functools.partial(attend_back_kernel, block, scale), grid=...]
    convert_element_type x76 -> x10, local copies, waits for them, and re-layouts: 190 us -> 1.38 us  [the longest x1 0.79 us: per_device(): softened.astype(BF)]
    while x192 -> x0, local copies, waits for them, and re-layouts: 188 us -> none
    reduce_scatter x8 -> x6, waiting for transfers between devices: 564 us -> 377 us  [the longest x5 364 us: owned(): lax.psum_scatter(grad.astype(BF), 'fsdp', scatter_dimension=axis, tiled=T...]
    all_gather x9 -> x11, waiting for transfers between devices: 175 us -> 349 us  [the longest x5 204 us: gather_rows(): return lax.all_gather(array, 'fsdp', axis=axis, tiled=True)]
    reshape x72 -> x9, local copies, waits for them, and re-layouts: 134 us -> 0.58 us  [per_device(): s.reshape(fsdp_count, -1)]
    mul x24 -> x0, local copies, waits for them, and re-layouts: 131 us -> none  [head_backward(): delta_pair = delta_weights * normalized]
  transfers between devices with their start and end apart: 19 -> 18, of which waited for: 11 -> 15; matrix products, arithmetic and copies ran while one was open for 42% -> 10% of each run, Pallas kernels for 0% -> 7%
where the time goes in v1:
time: 1240 us; the launch traced here: 1230 us
  waiting for transfers between devices  754 us (61%)
  Pallas kernels  192 us (15%)
  matrix products  93.7 us (8%)
  blocking collectives  75.9 us (6%)
  local copies, waits for them, and re-layouts  64.1 us (5%)
  other arithmetic  33.6 us (3%)
  between operations  15.6 us (1%)
    reduce_scatter x5, waiting for transfers between devices, owned(): lax.psum_scatter(grad.astype(BF), 'fsdp', scatter_dimension=axis, tiled=T...  364 us
    all_gather x5, waiting for transfers between devices, gather_rows(): return lax.all_gather(array, 'fsdp', axis=axis, tiled=True)  204 us
    all_gather x2, waiting for transfers between devices, own_tree(): whole = lax.all_gather(tokens[:, 0], 'leaf', axis=1, tiled=True)  92.8 us
    pallas_call x1, Pallas kernels, attend_back(): pl.pallas_call(functools.partial(attend_back_kernel, block, scale), grid=...  83.5 us
    pallas_call x6, Pallas kernels, reorder(): pl.pallas_call(reorder_kernel, name='reorder', grid_spec=pltpu.PrefetchSc...  63.6 us
    pallas_call x1, Pallas kernels, attend(): pl.pallas_call(functools.partial(attend_kernel, block), grid=(pairs,), na...  44.4 us
    all_gather x2, waiting for transfers between devices, own_tokens(): whole = lax.all_gather(halves, 'leaf', axis=0, tiled=True)  40.9 us
    unnamed x1, blocking collectives  37.7 us
  transfers between devices with their start and end apart: 18, of which 15 were waited for; matrix products, arithmetic and copies ran while one was open for 10% of the time, Pallas kernels for 7%

profile of v1, /device:TPU:0, one launch (start us, length us, event | category | flops | bytes accessed | tf_op | source)
XLA Modules:
  0.0 1229.7 jit_solution(12317709151530253201)
XLA Ops:
  15.7 32.5 %all-gather.3 = bf16[8,1,1152]{2,1,0:T(2,128)(2,1)S(1)} all-gather(bf16[1,1,1152]{2,1,0:T(2,128)(2,1)S(1)} %reshape.489), channel_id=3, replica_groups=mesh['leaf'=4,'fsdp'=8] {'fsdp'}, dimensions={0}, use_global_device_ids=true | all-gather | bytes 20736 | tf_op jit(solution)/shard_map/all_gather | solution.py:314
  49.2 29.2 %all-gather.16.cloned.1.call-done = bf16[768,2304]{1,0:T(8,128)(2,1)} async-done(((bf16[96,2304]{1,0:T(8,128)(2,1)}), bf16[768,2304]{1,0:T(8,128)(2,1)}) %all-gather.16.cloned.1.call-update) | async-done | bytes 3538960 | tf_op jit(solution)/shard_map/all_gather | solution.py:314
  80.0 44.8 %all-gather.34.cloned.1.call-done = bf16[2,1,2048,768]{3,2,1,0:T(8,128)(2,1)} async-done(((bf16[2,1,512,768]{3,2,1,0:T(8,128)(2,1)}), bf16[2,1,2048,768]{3,2,1,0:T(8,128)(2,1)}) %all-gather.34.cloned.1.call-update) | async-done | bytes 6291472 | tf_op jit(solution)/shard_map/all_gather | solution.py:357
  124.9 48.0 %all-gather.36.cloned.1.call-done = bf16[2,1,2048,768]{3,2,1,0:T(8,128)(2,1)} async-done(((bf16[2,1,512,768]{3,2,1,0:T(8,128)(2,1)}), bf16[2,1,2048,768]{3,2,1,0:T(8,128)(2,1)}) %all-gather.36.cloned.1.call-update) | async-done | bytes 6291472 | tf_op jit(solution)/shard_map/all_gather | solution.py:357
  172.9 5.9 constant_dynamic-slice_fusion.2
  178.8 10.5 reorder.6
  189.3 6.2 fusion.21
  197.5 38.6 %all-gather.18.cloned.1.call-done.mask_ref = bf16[6,512,512]{2,1,0:T(8,128)(2,1)} async-done(((bf16[6,64,512]{2,1,0:T(8,128)(2,1)}), bf16[6,512,512]{2,1,0:T(8,128)(2,1)}) %all-gather.18.cloned.1.call-update) | async-done | bytes 3145744 | tf_op jit(solution)/shard_map/all_gather | solution.py:314
  236.0 44.4 %attend.1 = (bf16[2048,384]{1,0:T(8,128)(2,1)S(1)}, f32[2048,384]{1,0:T(8,128)}) custom-call(bf16[2048,384]{1,0:T(8,128)(2,1)S(1)} %get-tuple-element.50.query_ref, bf16[2048,384]{1,0:T(8,128)(2,1)S(1)} %get-tuple-element.49.key_ref, bf16[2048,384]{1,0:T(8,128)(2,1)} %fusion.13.value_ref, bf16[6,512,512]{2,1,0:T(8,128)(2,1)} %all-gather.18.cloned.1.call-done.mask_ref), custom_call_target="tpu_custom_call" | custom-call | tf_op jit(solution)/shard_map/attend/pallas_call | solution.py:164
  287.0 10.6 reorder.9
  299.9 3.9 fusion.42
  305.9 69.8 %all-gather.24.cloned.1.call-done = bf16[768,3072]{1,0:T(8,128)(2,1)} async-done(((bf16[96,3072]{1,0:T(8,128)(2,1)}), bf16[768,3072]{1,0:T(8,128)(2,1)}) %all-gather.24.cloned.1.call-update) | async-done | bytes 4718608 | tf_op jit(solution)/shard_map/all_gather | solution.py:314
  375.7 13.4 %multiply_convert_fusion = (bf16[1024,3072]{1,0:T(8,128)(2,1)}, f32[1024,3072]{1,0:T(8,128)}) fusion(f32[3072]{0:T(1024)S(1)} %reshape.478, bf16[768,3072]{1,0:T(8,128)(2,1)} %all-gather.24.cloned.1.call-done, f32[1024,768]{0,1:T(8,128)} %copy-done.4, f32[768]{0:T(1024)S(1)} %reshape.477, f32[768]{0:T(1024)S(1)} %reshape.476, f32[1024]{0:T(1024)S(1)} %add_rsqrt_fusion.1, ...), kind=kOutput, calls=%fused_computation.8 | convolution fusion | flops 4854644736 | bytes 26765312 | tf_op jit(solution)/shard_map/dot_general | solution.py:45
  389.2 66.8 %all-gather.26.cloned.1.call-done = bf16[3072,768]{1,0:T(8,128)(2,1)} async-done(((bf16[384,768]{1,0:T(8,128)(2,1)}), bf16[3072,768]{1,0:T(8,128)(2,1)}) %all-gather.26.cloned.1.call-update) | async-done | bytes 4718608 | tf_op jit(solution)/shard_map/all_gather | solution.py:314
  456.0 9.4 fusion.43
  469.9 13.0 %convert_reduce_fusion = (f32[3072]{0:T(1024)S(1)}, bf16[1024,3072]{1,0:T(8,128)(2,1)S(1)}) fusion(f32[1024,3072]{1,0:T(8,128)} %get-tuple-element.80, f32[3072]{0:T(1024)S(1)} %reshape.478, bf16[1024,768]{0,1:T(8,128)(2,1)S(1)} %get-tuple-element.46, bf16[3072,768]{1,0:T(8,128)(2,1)S(1)} %bitcast.71), kind=kOutput, calls=%fused_computation.7 | convolution fusion | flops 4872729600 | bytes 25190400 | tf_op jit(solution)/shard_map/dot_general | solution.py:49
  482.9 6.7 multiply_reduce_fusion
  492.5 2.6 convolution_convert_fusion.4
  495.2 10.4 all-gather.30.cloned.1.call-done
  505.6 2.7 constant_dynamic-slice_fusion.delta_ref
  508.3 83.5 %attend_back.1 = (bf16[2048,384]{1,0:T(8,128)(2,1)S(1)}, bf16[2048,384]{1,0:T(8,128)(2,1)S(1)}, bf16[2048,384]{1,0:T(8,128)(2,1)S(1)}, f32[6,512,512]{2,1,0:T(8,128)}) custom-call(bf16[2048,384]{1,0:T(8,128)(2,1)} %copy-done.1, bf16[2048,384]{1,0:T(8,128)(2,1)} %copy-done, bf16[2048,384]{1,0:T(8,128)(2,1)} %fusion.13.value_ref, ...), custom_call_target="tpu_custom_call" | custom-call | tf_op jit(solution)/shard_map/attend_back/pallas_call | solution.py:276
  594.8 5.5 convolution_convert_fusion.3
  600.4 4.8 convert_element_type.279
  605.3 4.8 convolution_convert_fusion.5
  610.2 10.1 convolution_convert_fusion.1
  620.3 9.2 convolution_convert_fusion
  629.6 8.8 convolution_convert_fusion.2
  639.1 28.5 %reduce-scatter.9.cloned.1.call-done = bf16[96,1152]{1,0:T(8,128)(2,1)} async-done(((bf16[768,1152]{1,0:T(8,128)(2,1)}), bf16[96,1152]{1,0:T(8,128)(2,1)}) %reduce-scatter.9.cloned.1.call-update) | async-done | bytes 221200 | tf_op jit(solution)/shard_map/reduce_scatter | solution.py:487
  673.0 72.5 %reduce-scatter.17.cloned.1.call-done = bf16[6,64,512]{2,1,0:T(8,128)(2,1)} async-done(((bf16[6,512,512]{2,1,0:T(8,128)(2,1)}), bf16[6,64,512]{2,1,0:T(8,128)(2,1)}) %reduce-scatter.17.cloned.1.call-update) | async-done | bytes 393232 | tf_op jit(solution)/shard_map/reduce_scatter | solution.py:487
  748.3 64.8 %reduce-scatter.11.cloned.1.call-done = bf16[96,768]{1,0:T(8,128)(2,1)} async-done(((bf16[768,768]{1,0:T(8,128)(2,1)}), bf16[96,768]{1,0:T(8,128)(2,1)}) %reduce-scatter.11.cloned.1.call-update) | async-done | bytes 147472 | tf_op jit(solution)/shard_map/reduce_scatter | solution.py:487
  813.1 98.5 %reduce-scatter.13.cloned.1.call-done = bf16[96,3072]{1,0:T(8,128)(2,1)} async-done(((bf16[768,3072]{1,0:T(8,128)(2,1)}), bf16[96,3072]{1,0:T(8,128)(2,1)}) %reduce-scatter.13.cloned.1.call-update) | async-done | bytes 589840 | tf_op jit(solution)/shard_map/reduce_scatter | solution.py:487
  911.5 99.6 %reduce-scatter.15.cloned.1.call-done = bf16[384,768]{1,0:T(8,128)(2,1)} async-done(((bf16[3072,768]{1,0:T(8,128)(2,1)}), bf16[384,768]{1,0:T(8,128)(2,1)}) %reduce-scatter.15.cloned.1.call-update) | async-done | bytes 589840 | tf_op jit(solution)/shard_map/reduce_scatter | solution.py:487
  1011.2 12.8 %reduce-scatter.7.cloned.1.call-done = bf16[1024,768]{0,1:T(8,128)(2,1)} async-done(((bf16[2048,768]{0,1:T(8,128)(2,1)}), bf16[1024,768]{0,1:T(8,128)(2,1)}) %reduce-scatter.7.cloned.1.call-update) | async-done | bytes 1572880 | tf_op jit(solution)/shard_map/reduce_scatter | solution.py:472
  1023.9 4.1 add_convert_fusion
  1030.4 37.7 %all-reduce = f32[8,1152]{1,0:T(8,128)S(1)} all-reduce(f32[8,1152]{1,0:T(8,128)S(1)} %concatenate.17), channel_id=7, replica_groups=mesh['leaf'=4,'fsdp'=8] {'fsdp'}, use_global_device_ids=true, to_apply=%region_42.43.clone | all-reduce | flops 9216 | bytes 73728
  1068.7 5.8 psum.43
  1075.8 5.4 fusion.41
  1081.1 4.9 copy.65
  1086.0 10.5 reorder.8
  1096.5 2.8 copy.64
  1099.4 10.8 reorder.7
  1112.6 24.6 %all-reduce.4.cloned.1.call-done = (bf16[96,2304]{1,0:T(8,128)(2,1)}, bf16[96,768]{1,0:T(8,128)(2,1)}, bf16[96,3072]{1,0:T(8,128)(2,1)}, bf16[384,768]{1,0:T(8,128)(2,1)}, bf16[12,64,512]{2,1,0:T(8,128)(2,1)}) async-done(((bf16[96,2304]{1,0:T(8,128)(2,1)}, bf16[96,768]{1,0:T(8,128)(2,1)}, bf16[96,3072]{1,0:T(8,128)(2,1)}, bf16[384,768]{1,0:T(8,128)(2,1)}, bf16[12,64,512]{2,1,0:T(8,128)(2,1)}), ...) | async-done | bytes 2555920 | tf_op jit(solution)/shard_map/psum | solution.py:508
  1144.8 40.9 %all-gather.32.cloned.1.call-done = bf16[4096,768]{0,1:T(8,128)(2,1)} async-done(((bf16[1024,768]{0,1:T(8,128)(2,1)}), bf16[4096,768]{0,1:T(8,128)(2,1)}) %all-gather.32.cloned.1.call-update) | async-done | bytes 6291472 | tf_op jit(solution)/shard_map/all_gather | solution.py:362
  1185.8 5.4 fusion.40
  1191.2 4.7 copy.70
  1195.9 10.5 reorder.11
  1206.3 2.9 copy.69
  1209.2 10.8 reorder.10
  (226 shorter events, 59.6 us)
Async XLA Ops:
  7.2 71.2 %all-gather.16.cloned.1.call-start = ((), (), s32[]{:S(2)}) async-start(), calls=%async_computation.6 | async-start | bytes 3981312 | tf_op jit(solution)/shard_map/all_gather | solution.py:314
  8.0 116.9 %all-gather.34.cloned.1.call-start = ((), (), s32[]{:S(2)}) async-start(), calls=%async_computation.21 | async-start | bytes 7864320 | tf_op jit(solution)/shard_map/all_gather | solution.py:357
  8.7 164.2 %all-gather.36.cloned.1.call-start = ((), (), s32[]{:S(2)}) async-start(), calls=%async_computation.22 | async-start | bytes 7864320 | tf_op jit(solution)/shard_map/all_gather | solution.py:357
  9.4 226.6 %all-gather.18.cloned.1.call-start = ((), (), s32[]{:S(2)}) async-start(), calls=%async_computation.7 | async-start | bytes 3538944 | tf_op jit(solution)/shard_map/all_gather | solution.py:314
  9.5 6.0 copy-start.25
  9.6 6.0 copy-start.27
  9.6 6.0 copy-start.28
  9.6 6.0 copy-start.29
  9.6 6.0 copy-start.30
  9.6 6.0 copy-start.31
  9.6 6.0 copy-start.32
  9.6 6.0 copy-start.33
  9.6 6.0 copy-start.34
  12.2 287.7 %all-gather.22.cloned.1.call-start = ((), (), s32[]{:S(2)}) async-start(), calls=%async_computation.9 | async-start | bytes 1327104 | tf_op jit(solution)/shard_map/all_gather | solution.py:314
  12.7 287.1 %all-gather.20.cloned.1.call-start = ((), (), s32[]{:S(2)}) async-start(), calls=%async_computation.8 | async-start | bytes 4718592 | tf_op jit(solution)/shard_map/all_gather | solution.py:426
  48.5 130.3 %copy-start.22 = (s32[16]{0:T(128)}, s32[16]{0:T(128)S(1)}, u32[]{:S(2)}) copy-start(s32[16]{0:T(128)S(1)} %fusion.30.order_ref) | copy-start | bytes 196
  48.6 130.2 %copy-start.21 = (s32[16]{0:T(128)}, s32[16]{0:T(128)S(1)}, u32[]{:S(2)}) copy-start(s32[16]{0:T(128)S(1)} %fusion.29.order_ref) | copy-start | bytes 196
  80.0 109.3 %copy-start.15 = (bf16[768,384]{1,0:T(8,128)(2,1)}, bf16[768,384]{1,0:T(8,128)(2,1)S(1)}, u32[]{:S(2)}) copy-start(bf16[768,384]{1,0:T(8,128)(2,1)S(1)} %get-tuple-element.55) | copy-start | bytes 1769476
  80.0 109.3 %copy-start.16 = (bf16[768,384]{1,0:T(8,128)(2,1)}, bf16[768,384]{1,0:T(8,128)(2,1)S(1)}, u32[]{:S(2)}) copy-start(bf16[768,384]{1,0:T(8,128)(2,1)S(1)} %get-tuple-element.56) | copy-start | bytes 1769476
  80.0 109.3 %copy-start.17 = (bf16[768,384]{1,0:T(8,128)(2,1)}, bf16[768,384]{1,0:T(8,128)(2,1)S(1)}, u32[]{:S(2)}) copy-start(bf16[768,384]{1,0:T(8,128)(2,1)S(1)} %get-tuple-element.57) | copy-start | bytes 1769476
  197.4 83.0 %copy-start = (bf16[2048,384]{1,0:T(8,128)(2,1)}, bf16[2048,384]{1,0:T(8,128)(2,1)S(1)}, u32[]{:S(2)}) copy-start(bf16[2048,384]{1,0:T(8,128)(2,1)S(1)} %get-tuple-element.49.key_ref) | copy-start | bytes 4718596
  197.4 83.0 %copy-start.1 = (bf16[2048,384]{1,0:T(8,128)(2,1)}, bf16[2048,384]{1,0:T(8,128)(2,1)S(1)}, u32[]{:S(2)}) copy-start(bf16[2048,384]{1,0:T(8,128)(2,1)S(1)} %get-tuple-element.50.query_ref) | copy-start | bytes 4718596
  281.6 94.1 %all-gather.24.cloned.1.call-start = ((), (), s32[]{:S(2)}) async-start(), calls=%async_computation.10 | async-start | bytes 5308416 | tf_op jit(solution)/shard_map/all_gather | solution.py:314
  282.4 173.6 %all-gather.26.cloned.1.call-start = ((), (), s32[]{:S(2)}) async-start(), calls=%async_computation.11 | async-start | bytes 5308416 | tf_op jit(solution)/shard_map/all_gather | solution.py:314
  283.1 222.4 %all-gather.30.cloned.1.call-start = ((), (), s32[]{:S(2)}) async-start(), calls=%async_computation.13 | async-start | bytes 4718592 | tf_op jit(solution)/shard_map/all_gather | solution.py:456
  465.4 4.5 slice-start.2
  467.2 15.7 %slice-start = ((s8[4718592]{0:T(1024)(128)(4,1)}), s8[4194304]{0:T(1024)(128)(4,1)S(1)}, s32[]{:S(2)}) async-start(s8[4718592]{0:T(1024)(128)(4,1)} %bitcast.68), calls=%async_computation.24 | async-start | bytes 8388608
  469.8 13.0 %copy-start.13 = (bf16[1024,768]{0,1:T(8,128)(2,1)}, bf16[1024,768]{0,1:T(8,128)(2,1)S(1)}, u32[]{:S(2)}) copy-start(bf16[1024,768]{0,1:T(8,128)(2,1)S(1)} %get-tuple-element.46) | copy-start | bytes 4718596
  469.9 13.0 %copy-start.5 = (f32[1024,768]{0,1:T(8,128)S(1)}, f32[1024,768]{0,1:T(8,128)}, u32[]{:S(2)}) copy-start(f32[1024,768]{0,1:T(8,128)} %copy-done.4) | copy-start | bytes 9437188
  469.9 13.0 %slice-start.1 = ((s8[4718592]{0:T(1024)(128)(4,1)}), s8[524288]{0:T(1024)(128)(4,1)S(1)}, s32[]{:S(2)}) async-start(s8[4718592]{0:T(1024)(128)(4,1)} %bitcast.68), calls=%async_computation.25 | async-start | bytes 1048576
  482.9 6.7 copy-start.37
  495.2 172.5 %reduce-scatter.9.cloned.1.call-start = ((), (), s32[]{:S(2)}) async-start(), calls=%async_computation.16 | async-start | bytes 1990656 | tf_op jit(solution)/shard_map/reduce_scatter | solution.py:487
  600.3 145.2 %reduce-scatter.17.cloned.1.call-start = ((), (), s32[]{:S(2)}) async-start(), calls=%async_computation.20 | async-start | bytes 3538944 | tf_op jit(solution)/shard_map/reduce_scatter | solution.py:487
  605.2 207.9 %reduce-scatter.11.cloned.1.call-start = ((), (), s32[]{:S(2)}) async-start(), calls=%async_computation.17 | async-start | bytes 1327104 | tf_op jit(solution)/shard_map/reduce_scatter | solution.py:487
  610.1 301.4 %reduce-scatter.13.cloned.1.call-start = ((), (), s32[]{:S(2)}) async-start(), calls=%async_computation.18 | async-start | bytes 5308416 | tf_op jit(solution)/shard_map/reduce_scatter | solution.py:487
  620.3 390.8 %reduce-scatter.15.cloned.1.call-start = ((), (), s32[]{:S(2)}) async-start(), calls=%async_computation.19 | async-start | bytes 5308416 | tf_op jit(solution)/shard_map/reduce_scatter | solution.py:487
  629.6 394.4 %reduce-scatter.7.cloned.1.call-start = ((), (), s32[]{:S(2)}) async-start(), calls=%async_computation.14 | async-start | bytes 4718592 | tf_op jit(solution)/shard_map/reduce_scatter | solution.py:472
  638.5 437.3 %all-gather.28.cloned.1.call-start = ((), (), s32[]{:S(2)}) async-start(), calls=%async_computation.12 | async-start | bytes 7864320 | tf_op jit(solution)/shard_map/all_gather | solution.py:362
  639.1 498.1 %all-reduce.4.cloned.1.call-start = ((), (), s32[]{:S(2)}) async-start(), calls=%async_computation.23 | async-start | bytes 5111808 | tf_op jit(solution)/shard_map/psum | solution.py:508
  1011.1 16.9 %copy-start.36 = (u32[32]{0:T(128)S(1)}, u32[32]{0:T(128)}, u32[]{:S(2)}) copy-start(u32[32]{0:T(128)} %constant.113) | copy-start | bytes 388
  1011.1 174.6 %all-gather.32.cloned.1.call-start = ((), (), s32[]{:S(2)}) async-start(), calls=%async_computation.15 | async-start | bytes 7864320 | tf_op jit(solution)/shard_map/all_gather | solution.py:362
  1099.4 10.8 copy-start.7
  1112.6 30.7 %copy-start.9 = (f32[12,64,512]{2,1,0:T(8,128)S(1)}, f32[12,64,512]{2,1,0:T(8,128)}, u32[]{:S(2)}) copy-start(f32[12,64,512]{2,1,0:T(8,128)} %copy-done.8) | copy-start | bytes 4718596
  1112.6 30.7 %copy-start.24 = (f32[12]{0:T(128)S(1)}, f32[12]{0:T(128)}, u32[]{:S(2)}) copy-start(f32[12]{0:T(128)} %param.24) | copy-start | bytes 148
  1137.1 4.4 copy-start.19
  1137.1 5.4 copy-start.20
  1137.1 6.2 copy-start.14
  1209.2 10.8 copy-start.6
  (12 other events, 26.7 us)
Sparse Core Ops, SparseCore 0:
  10.2 68.1 all-gather.15
  79.9 44.8 all-gather.33
  126.4 46.3 all-gather.35
  175.5 60.5 all-gather.17
  238.1 39.6 all-gather.21
  281.8 10.6 all-gather.19
  294.6 81.0 all-gather.23
  377.9 78.0 all-gather.25
  495.3 10.2 all-gather.29
  600.4 67.1 reduce-scatter.8
  671.7 73.8 reduce-scatter.16
  749.8 63.2 reduce-scatter.10
  817.1 94.3 reduce-scatter.12
  915.5 95.5 reduce-scatter.14
  1013.3 10.6 reduce-scatter.6
  1025.9 47.5 all-gather.27
  1077.2 59.8 all-reduce.3
  1139.2 46.5 all-gather.31

commit v2 on v1

--- a/solution.py
+++ b/solution.py
@@ -310,6 +310,1157 @@
     )(order, tokens)
 
 
+MESH = pl.DeviceIdType.MESH
+ANY = pl.BlockSpec(memory_space=pl.ANY)
+VMEM = pl.BlockSpec(memory_space=pltpu.VMEM)
+SMEM = pl.BlockSpec(memory_space=pltpu.SMEM)
+VMEM_LIMIT = 60 << 20
+LINE = 4
+ALL = slice(None)
+
+
+class Net:
+    def __init__(self, send, recv, local):
+        leaf, shard = lax.axis_index("leaf"), lax.axis_index("fsdp")
+        self.leaf, self.shard = leaf, shard
+        self.x, self.c = leaf // 2, leaf % 2
+        self.z, self.y = shard // 2, shard % 2
+        self.send, self.recv, self.local = send, recv, local
+
+    def near(self, which):
+        x, c, y, z = self.x, self.c, self.y, self.z
+        if which == "x":
+            x = 1 - x
+        elif which == "c":
+            c = 1 - c
+        elif which == "xc":
+            x, c = 1 - x, 1 - c
+        elif which == "y":
+            y = 1 - y
+        else:
+            z = (z + which) % LINE
+        return (x * 2 + c, z * 2 + y)
+
+    def greet(self, peers):
+        barrier = pltpu.get_barrier_semaphore()
+        for peer in peers:
+            pl.semaphore_signal(barrier, inc=1, device_id=self.near(peer), device_id_type=MESH)
+        pl.semaphore_wait(barrier, len(peers))
+
+    def remote(self, row, slot, source, target, peer):
+        return pltpu.make_async_remote_copy(
+            src_ref=source,
+            dst_ref=target,
+            send_sem=self.send.at[row, slot],
+            recv_sem=self.recv.at[row, slot],
+            device_id=self.near(peer),
+            device_id_type=MESH,
+        )
+
+    def stay(self, row, source, target):
+        return pltpu.make_async_copy(source, target, self.local.at[row])
+
+
+class Gather:
+    def __init__(self, net, row, own, whole, share):
+        self.net, self.row, self.own, self.whole, self.share = net, row, own, whole, share
+
+    def copy(self, slot):
+        net, whole = self.net, self.whole
+        x, y, z = net.x, net.y, net.z
+        if slot < 3:
+            return net.remote(self.row, slot, self.own(x), whole(z, y, x), slot + 1)
+        if slot < 6:
+            piece = whole((z + LINE - (slot - 2)) % LINE, y, x)
+            return net.remote(self.row, slot, piece, piece, "x")
+        if slot == 6:
+            piece, peer = whole(ALL, y, x), "y"
+        elif slot == 7:
+            piece, peer = whole(slice(0, 2), 1 - y, x), "x"
+        elif slot == 8:
+            piece, peer = whole(slice(2, 4), y, 1 - x), "y"
+        else:
+            piece, peer = whole(ALL, ALL, ALL), "c"
+        return net.remote(self.row, slot, piece, piece, peer)
+
+    def home(self):
+        return self.net.stay(self.row, self.own(ALL), self.whole(self.net.z, self.net.y, ALL))
+
+    def step(self, number):
+        if number == 0:
+            self.home().start()
+            for slot in range(3):
+                self.copy(slot).start()
+        elif number == 1:
+            self.home().wait()
+            for slot in range(3):
+                self.copy(slot).wait_recv()
+            for slot in range(3, 7):
+                self.copy(slot).start()
+        elif number == 2:
+            for slot in range(3, 7):
+                self.copy(slot).wait_recv()
+            for slot in (7, 8):
+                self.copy(slot).start()
+        elif number == 3:
+            for slot in (7, 8):
+                self.copy(slot).wait_recv()
+            if self.share:
+                self.copy(9).start()
+        elif number == 4:
+            if self.share:
+                self.copy(9).wait_recv()
+
+    def finish(self):
+        for slot in range(10 if self.share else 9):
+            self.copy(slot).wait_send()
+
+
+class Scatter:
+    def __init__(self, net, row, load, part, twin, twin_load, first, second, third, final):
+        self.net, self.row, self.load, self.part = net, row, load, part
+        self.twin, self.twin_load = twin, twin_load
+        self.first, self.second, self.third, self.final = first, second, third, final
+
+    def copy(self, slot):
+        net, part = self.net, self.part
+        x, y, z, c = net.x, net.y, net.z, net.c
+        if slot == 0:
+            return net.remote(self.row, slot, self.twin_load, self.twin, "c")
+        if slot == 1:
+            return net.remote(self.row, slot, part.at[0:1, 1 - y, 1 - x], self.first.at[0:1], "x")
+        if slot == 2:
+            return net.remote(self.row, slot, part.at[1:4, 1 - y, 1 - x], self.first.at[1:4], "y")
+        if slot == 3:
+            return net.remote(self.row, slot, part.at[:, y, 1 - x], self.second.at[0], "x")
+        if slot == 4:
+            return net.remote(self.row, slot, part.at[:, 1 - y, x], self.second.at[1], "y")
+        if slot < 8:
+            step = slot - 4
+            piece = part.at[(z + step) % LINE, y, x]
+            return net.remote(self.row, slot, piece, self.third.at[step - 1], step)
+        peer = ("x", "c", "xc")[slot - 8]
+        return net.remote(self.row, slot, part.at[z, y, x], self.final(x, c), peer)
+
+    def home(self):
+        return self.net.stay(self.row, self.load, self.part)
+
+    def keep(self):
+        net = self.net
+        piece = self.part.at[net.z, net.y, net.x]
+        return net.stay(self.row, piece, self.final(net.x, net.c))
+
+    def step(self, number):
+        net, part = self.net, self.part
+        x, y, z = net.x, net.y, net.z
+        if number == 0:
+            if self.load is not None:
+                self.home().start()
+            if self.twin is not None:
+                self.copy(0).start()
+        elif number == 1:
+            if self.load is not None:
+                self.home().wait()
+            if self.twin is not None:
+                self.copy(0).wait_recv()
+                for a in range(LINE):
+                    part[a] = (part[a].astype(F32) + self.twin[a].astype(F32)).astype(BF)
+            self.copy(1).start()
+            self.copy(2).start()
+        elif number == 2:
+            self.copy(1).wait_recv()
+            other = part[0, 1 - y, x].astype(F32) + self.first[0].astype(F32)
+            part[0, 1 - y, x] = other.astype(BF)
+            self.copy(2).wait_recv()
+            other = part[1:4, y, 1 - x].astype(F32) + self.first[1:4].astype(F32)
+            part[1:4, y, 1 - x] = other.astype(BF)
+            self.copy(3).start()
+            self.copy(4).start()
+        elif number == 3:
+            self.copy(3).wait_recv()
+            self.copy(4).wait_recv()
+            mine = part[:, y, x].astype(F32) + self.second[0].astype(F32)
+            part[:, y, x] = (mine + self.second[1].astype(F32)).astype(BF)
+            for slot in (5, 6, 7):
+                self.copy(slot).start()
+        elif number == 4:
+            total = part[z, y, x].astype(F32)
+            for slot in (5, 6, 7):
+                self.copy(slot).wait_recv()
+                total = total + self.third[slot - 5].astype(F32)
+            part[z, y, x] = total.astype(BF)
+            for slot in (8, 9, 10):
+                self.copy(slot).start()
+            self.keep().start()
+        elif number == 5:
+            self.keep().wait()
+            for slot in (8, 9, 10):
+                self.copy(slot).wait_recv()
+
+    def finish(self):
+        for slot in range(0 if self.twin is not None else 1, 11):
+            self.copy(slot).wait_send()
+
+
+def copy_semaphores(rows, slots):
+    return [
+        pltpu.SemaphoreType.DMA((rows, slots)),
+        pltpu.SemaphoreType.DMA((rows, slots)),
+        pltpu.SemaphoreType.DMA((rows,)),
+    ]
+
+
+def run_plan(plan, slot, total):
+    for number in range(total):
+        steps = [entry for entry in plan if int(entry[0]) == number]
+        if steps:
+
+            @pl.when(slot == number)
+            def _(steps=steps):
+                for _, chunk, step in steps:
+                    chunk.step(step)
+
+
+def run_rest(plan, total):
+    for time, chunk, step in plan:
+        if time >= total:
+            chunk.step(step)
+
+
+def enter_kernel(
+    tokens_ref, joined_ref, mask_ref, vectors_ref, tree_ref, weight_ref, heads_ref, packed_ref, *sems
+):
+    net = Net(*sems)
+    x, c, y, z, leaf = net.x, net.c, net.y, net.z, net.leaf
+    piece = joined_ref.shape[2] // 6
+    chunks = []
+    for i in range(3):
+        source = pl.ds(pl.multiple_of((2 * i + c) * piece, piece), piece)
+        target = pl.ds(i * piece, piece)
+        chunks.append(
+            Gather(
+                net,
+                i,
+                lambda half, source=source: joined_ref.at[half, :, source],
+                lambda a, b, half, target=target: weight_ref.at[a, b, half, :, target],
+                False,
+            )
+        )
+    for i in range(2):
+        head = c * (mask_ref.shape[0] // 2) + i
+        chunks.append(
+            Gather(
+                net,
+                3 + i,
+                lambda half, head=head: mask_ref.at[head, half],
+                lambda a, b, half, i=i: heads_ref.at[i, a, b, half],
+                False,
+            )
+        )
+    net.greet(("x", "c", "y", 1, 2, 3))
+    row = len(chunks)
+    half_rows = tokens_ref.shape[1] // 2
+    other = (leaf + 2) % 4
+
+    def token_copy(slot):
+        part = pl.ds((slot % 2) * half_rows, half_rows)
+        if slot < 2:
+            return net.remote(row, slot, tokens_ref.at[1 - x, part], tree_ref.at[leaf, part], "x")
+        if slot < 4:
+            return net.remote(row, slot, tokens_ref.at[x, part], tree_ref.at[leaf, part], "c")
+        place = tree_ref.at[other, part]
+        return net.remote(row, slot, place, place, "c")
+
+    def vector_copy(slot):
+        if slot < 3:
+            return net.remote(row + 1, slot, vectors_ref, packed_ref.at[z, y], slot + 1)
+        return net.remote(row + 1, slot, packed_ref.at[:, y], packed_ref.at[:, y], "y")
+
+    keep_tokens = net.stay(row, tokens_ref.at[x], tree_ref.at[leaf])
+    keep_vectors = net.stay(row + 1, vectors_ref, packed_ref.at[z, y])
+    for slot in range(2):
+        token_copy(slot).start()
+    for slot in range(3):
+        vector_copy(slot).start()
+    keep_vectors.start()
+    keep_tokens.start()
+    chunks[0].step(0)
+    chunks[1].step(0)
+    for slot in (2, 3):
+        token_copy(slot).start()
+    for time in range(len(chunks) + 2):
+        if time < len(chunks):
+            chunks[time].step(1)
+        if 0 <= time - 2 < len(chunks):
+            chunks[time - 2].step(2)
+        if time + 2 < len(chunks):
+            chunks[time + 2].step(0)
+        if time == 1:
+            keep_vectors.wait()
+            for slot in range(3):
+                vector_copy(slot).wait_recv()
+            vector_copy(3).start()
+        if time == 3:
+            token_copy(0).wait_recv()
+            token_copy(4).start()
+    for chunk in chunks:
+        chunk.step(3)
+    token_copy(1).wait_recv()
+    token_copy(5).start()
+    for slot in (2, 3, 4, 5):
+        token_copy(slot).wait_recv()
+    vector_copy(3).wait_recv()
+    keep_tokens.wait()
+    for chunk in chunks:
+        chunk.finish()
+    for slot in range(6):
+        token_copy(slot).wait_send()
+    for slot in range(4):
+        vector_copy(slot).wait_send()
+
+
+def enter(tokens, joined, mask, vectors):
+    micro, rows, width = tokens.shape
+    heads, _, strip, span = mask.shape
+    _, half, columns = joined.shape
+    return pl.pallas_call(
+        enter_kernel,
+        name="enter",
+        in_specs=[ANY] * 4,
+        out_specs=[VMEM] * 4,
+        out_shape=[
+            jax.ShapeDtypeStruct((4, rows, width), BF),
+            jax.ShapeDtypeStruct((LINE, 2, 2, half, columns // 2), BF),
+            jax.ShapeDtypeStruct((2, LINE, 2, 2, strip, span), BF),
+            jax.ShapeDtypeStruct((LINE, 2) + vectors.shape, vectors.dtype),
+        ],
+        scratch_shapes=copy_semaphores(7, 9),
+        compiler_params=pltpu.CompilerParams(
+            collective_id=0, has_side_effects=True, vmem_limit_bytes=VMEM_LIMIT
+        ),
+    )(tokens, joined, mask, vectors)
+
+
+def joined_kernel(
+    order_ref, tree_ref, weight_ref, query_bias_ref, value_bias_ref, tokens_ref, query_ref, key_ref, value_ref, sems
+):
+    blocks, block, width = tokens_ref.shape
+    mine = query_ref.shape[1]
+    per = tree_ref.shape[1] // block
+
+    def copy(i):
+        place = order_ref[i]
+        rows = pl.ds(pl.multiple_of((place % per) * block, block), block)
+        return pltpu.make_async_copy(tree_ref.at[place // per, rows], tokens_ref.at[i], sems.at[i])
+
+    for i in range(blocks):
+        copy(i).start()
+
+    def project(i, carry):
+        copy(2 * i).wait()
+        copy(2 * i + 1).wait()
+        pair = tokens_ref[pl.ds(2 * i, 2)].reshape(2 * block, width)
+        rows = pl.ds(pl.multiple_of(2 * block * i, 2 * block), 2 * block)
+        joined = dot_nn(pair, weight_ref[...])
+        query = (joined[:, :mine] + query_bias_ref[...]).astype(BF).astype(F32)
+        query_ref[rows, :] = (query * (1.0 / math.sqrt(LOW_HALF))).astype(BF)
+        key_ref[rows, :] = joined[:, mine : 2 * mine].astype(BF)
+        value_ref[rows, :] = (joined[:, 2 * mine :] + value_bias_ref[...]).astype(BF)
+        return carry
+
+    lax.fori_loop(0, blocks // 2, project, 0)
+
+
+def join(order, tree, weight, query_bias, value_bias):
+    parts, rows, width = tree.shape
+    blocks = order.shape[0]
+    block = parts * rows // blocks
+    mine = weight.shape[1] // 3
+    return pl.pallas_call(
+        joined_kernel,
+        name="join",
+        in_specs=[SMEM, ANY, VMEM, VMEM, VMEM],
+        out_specs=[VMEM] * 4,
+        out_shape=[jax.ShapeDtypeStruct((blocks, block, width), BF)]
+        + [jax.ShapeDtypeStruct((parts * rows, mine), BF)] * 3,
+        scratch_shapes=[pltpu.SemaphoreType.DMA((blocks,))],
+        compiler_params=pltpu.CompilerParams(vmem_limit_bytes=VMEM_LIMIT),
+    )(order, tree, weight, query_bias, value_bias)
+
+
+def pick_kernel(order_ref, tree_ref, out_ref, sems):
+    count, block, _ = out_ref.shape
+    per = tree_ref.shape[1] // block
+    copies = []
+    for i in range(count):
+        place = order_ref[i]
+        rows = pl.ds(pl.multiple_of((place % per) * block, block), block)
+        copies.append(
+            pltpu.make_async_copy(tree_ref.at[place // per, rows], out_ref.at[i], sems.at[i])
+        )
+    for copy in copies:
+        copy.start()
+    for copy in copies:
+        copy.wait()
+
+
+def pick(order, tree, block):
+    count = order.shape[0]
+    return pl.pallas_call(
+        pick_kernel,
+        name="pick",
+        in_specs=[SMEM, ANY],
+        out_specs=VMEM,
+        out_shape=jax.ShapeDtypeStruct((count, block, tree.shape[2]), tree.dtype),
+        scratch_shapes=[pltpu.SemaphoreType.DMA((count,))],
+        compiler_params=pltpu.CompilerParams(vmem_limit_bytes=VMEM_LIMIT),
+    )(order, tree)
+
+
+class Sharing:
+    def __init__(self, net, row, own, tree):
+        self.net, self.row, self.own, self.tree = net, row, own, tree
+
+    def copy(self, slot):
+        net, own, tree = self.net, self.own, self.tree
+        half = own.shape[1] // 2
+        part = pl.ds((slot % 2) * half, half)
+        if slot < 2:
+            return net.remote(self.row, slot, own.at[1 - net.x, part], tree.at[net.leaf, part], "x")
+        if slot < 4:
+            return net.remote(self.row, slot, own.at[net.x, part], tree.at[net.leaf, part], "c")
+        place = tree.at[(net.leaf + 2) % 4, part]
+        return net.remote(self.row, slot, place, place, "c")
+
+    def home(self):
+        return self.net.stay(self.row, self.own.at[self.net.x], self.tree.at[self.net.leaf])
+
+    def step(self, number):
+        if number == 0:
+            for slot in range(4):
+                self.copy(slot).start()
+            self.home().start()
+        elif number < 3:
+            self.copy(number - 1).wait_recv()
+            self.copy(number + 3).start()
+        elif number == 3:
+            for slot in (2, 3, 4, 5):
+                self.copy(slot).wait_recv()
+            self.home().wait()
+
+    def finish(self):
+        for slot in range(6):
+            self.copy(slot).wait_send()
+
+
+ATTEND_PLAN = (1.9, 1.5, 3.0, 3.0, 3.0)
+
+
+def attend_wide_kernel(
+    block,
+    query_ref,
+    key_ref,
+    value_ref,
+    first_ref,
+    relaxed_ref,
+    out_shard,
+    up_shard,
+    down_shard,
+    upstream_ref,
+    attended_ref,
+    log_ref,
+    whole_ref,
+    mask_ref,
+    out_weight,
+    up_weight,
+    down_weight,
+    tree_ref,
+    *sems,
+):
+    net = Net(*sems)
+    c = net.c
+    trunk = TRUNK * block
+    wide = 3 * block
+    low = low_lanes()
+    rows_all, width_all = query_ref.shape
+    pairs = width_all // (2 * LOW_HALF)
+    heads = relaxed_ref.shape[0] // 2
+    half = rows_all // 2
+    piece = out_shard.shape[2] // 2
+    chunks = []
+    for h in range(2, heads):
+        head = c * heads + h
+        chunks.append(
+            Gather(
+                net,
+                len(chunks),
+                lambda part, head=head: relaxed_ref.at[head, part],
+                lambda a, b, part, h=h: mask_ref.at[h, a, b, part],
+                False,
+            )
+        )
+    columns = pl.ds(pl.multiple_of(c * piece, piece), piece)
+    chunks.append(
+        Gather(
+            net,
+            len(chunks),
+            lambda part: out_shard.at[part, :, columns],
+            lambda a, b, part: out_weight.at[a, b, part, :, columns],
+            True,
+        )
+    )
+    for j in range(4):
+        place = pl.ds(pl.multiple_of((4 * c + j) * piece, piece), piece)
+        chunks.append(
+            Gather(
+                net,
+                len(chunks),
+                lambda part, place=place: up_shard.at[part, :, place],
+                lambda a, b, part, place=place: up_weight.at[a, b, part, :, place],
+                True,
+            )
+        )
+    for j in range(4):
+        chunks.append(
+            Gather(
+                net,
+                len(chunks),
+                lambda part, j=j: down_shard.at[j, part, :, columns],
+                lambda a, b, part, j=j: down_weight.at[a, b, j, part, :, columns],
+                True,
+            )
+        )
+    share = Sharing(net, len(chunks), upstream_ref, tree_ref)
+    net.greet(("x", "c", "y", 1, 2, 3))
+    first_copy = net.stay(len(chunks) + 1, first_ref, mask_ref.at[0:2])
+    first_copy.start()
+    total = 8 * pairs
+    plan = []
+    pace, lead, lag1, lag2, lag3 = ATTEND_PLAN
+    for i, chunk in enumerate(chunks):
+        start = i * pace
+        plan.append((max(0.0, start - lead), chunk, 0))
+        start = start + lag1
+        for step in (1, 2, 3, 4):
+            plan.append((start, chunk, step))
+            start = start + (lag2, lag3, lag3, lag3)[step - 1]
+    for i in range(4):
+        plan.append(((4 + 3 * i) * pace, share, i))
+    fixed = []
+    for time, chunk, step in plan:
+        for h in range(2, heads):
+            if chunk is chunks[h - 2]:
+                time = min(time, 8 * (h // 2) - 0.01 * (4 - step))
+        fixed.append((time, chunk, step))
+    plan = sorted(fixed, key=lambda entry: entry[0])
+    first_copy.wait()
+
+    def soften(parts, masks, values):
+        top = parts[0].max(axis=1, keepdims=True)
+        for part in parts[1:]:
+            top = jnp.maximum(top, part.max(axis=1, keepdims=True))
+        scale = 0.0
+        out = 0.0
+        for part, mask, value in zip(parts, masks, values):
+            weight = jnp.exp(part - top)
+            scale = scale + weight.sum(axis=1, keepdims=True)
+            out = out + dot_nn((weight * mask.astype(F32)).astype(BF), value)
+        return (out * (1.0 / scale), top + jnp.log(scale))
+
+    def emit(rows, lanes, results):
+        count = results[0][1].shape[0]
+        attended_ref[rows, lanes] = jnp.where(low, results[0][0], results[1][0]).astype(BF)
+        logs = [jnp.broadcast_to(result[1], (count, 2 * LOW_HALF)) for result in results]
+        log_ref[rows, lanes] = jnp.where(low, logs[0], logs[1])
+
+    def one_pair(p, carry):
+        lanes = pl.ds(pl.multiple_of(p * 2 * LOW_HALF, 2 * LOW_HALF), 2 * LOW_HALF)
+
+        def mask_strip(which, tile):
+            return mask_ref[2 * p + which, tile].reshape(block, mask_ref.shape[-1])
+
+        def trunk_rows(index, carry):
+            run_plan(plan, 8 * p + index, total)
+            rows = pl.ds(pl.multiple_of(index * block, block), block)
+            query = query_ref[rows, lanes]
+            results = []
+            for which in range(2):
+                mask_rows = mask_strip(which, index)
+                columns = [(0, trunk, mask_rows)]
+                side = mask_columns(mask_rows, (1, 0, 1), block)
+                columns += [(trunk + wide * g, wide, side) for g in range(GROUPS)]
+                head = one_head(query, which)
+                parts = [dot_nt(head, key_ref[a : a + w, lanes]) for a, w, _ in columns]
+                values = [value_ref[a : a + w, lanes] for a, w, _ in columns]
+                results.append(soften(parts, [column[2] for column in columns], values))
+            emit(rows, lanes, results)
+            return carry
+
+        lax.fori_loop(0, TRUNK, trunk_rows, 0)
+
+        def group_rows(group, carry):
+            run_plan(plan, 8 * p + 4 + group, total)
+            base = pl.multiple_of(trunk + wide * group, block)
+            for row in range(3):
+                rows = pl.ds(pl.multiple_of(base + block * row, block), block)
+                query = query_ref[rows, lanes]
+                tile = 0 if row == 1 else 1
+                start, width, tiles = group_columns(row, block)
+                columns = pl.ds(pl.multiple_of(base + start, block), width)
+                results = []
+                for which in range(2):
+                    mask_rows = mask_strip(which, tile)
+                    head = one_head(query, which)
+                    parts = [
+                        dot_nt(head, key_ref[0:trunk, lanes]),
+                        dot_nt(head, key_ref[columns, lanes]),
+                    ]
+                    masks = [mask_rows, mask_columns(mask_rows, tiles, block)]
+                    values = [value_ref[0:trunk, lanes], value_ref[columns, lanes]]
+                    results.append(soften(parts, masks, values))
+                emit(rows, lanes, results)
+            return carry
+
+        lax.fori_loop(0, GROUPS, group_rows, 0)
+        return carry
+
+    lax.fori_loop(0, pairs, one_pair, 0)
+    mine = pl.ds(pl.multiple_of(c * half, half), half)
+    theirs = pl.ds(pl.multiple_of((1 - c) * half, half), half)
+    place = pl.ds(pl.multiple_of(c * width_all, width_all), width_all)
+    cross = net.remote(
+        len(chunks) + 1, 0, attended_ref.at[theirs], whole_ref.at[:, place], "c"
+    )
+    cross.start()
+    whole_ref[:, place] = attended_ref[mine, :]
+    run_rest(plan, total)
+    cross.wait_recv()
+    for chunk in chunks + [share]:
+        chunk.finish()
+    cross.wait_send()
+
+
+def attend_wide(query, key, value, first, relaxed, out_shard, up_shard, down_shard, upstream, block):
+    rows, width = query.shape
+    heads = relaxed.shape[0] // 2
+    grown = lambda shard: jax.ShapeDtypeStruct((LINE, 2) + shard.shape, BF)
+    return pl.pallas_call(
+        functools.partial(attend_wide_kernel, block),
+        name="attend_wide",
+        in_specs=[VMEM] * 3 + [ANY] * 6,
+        out_specs=[VMEM] * 8,
+        out_shape=[
+            jax.ShapeDtypeStruct((rows, width), BF),
+            jax.ShapeDtypeStruct((rows, width), F32),
+            jax.ShapeDtypeStruct((rows // 2, 2 * width), BF),
+            jax.ShapeDtypeStruct((heads,) + first.shape[1:], BF),
+            grown(out_shard),
+            grown(up_shard),
+            grown(down_shard),
+            jax.ShapeDtypeStruct((4,) + upstream.shape[1:], BF),
+        ],
+        scratch_shapes=copy_semaphores(15, 10),
+        compiler_params=pltpu.CompilerParams(
+            collective_id=1, has_side_effects=True, vmem_limit_bytes=VMEM_LIMIT
+        ),
+    )(query, key, value, first, relaxed, out_shard, up_shard, down_shard, upstream)
+
+
+BACK_PLAN = (1.6, 1.0, 1.6, 1.6, 1.6, 1.6)
+
+
+def attend_back_wide_kernel(
+    block,
+    scale,
+    query_ref,
+    key_ref,
+    value_ref,
+    mask_ref,
+    out_ref,
+    log_ref,
+    delta_half,
+    layer_half,
+    place_ref,
+    out_grad,
+    up_grad,
+    down_grad,
+    dquery_ref,
+    dkey_ref,
+    dvalue_ref,
+    last_ref,
+    out_final,
+    up_final,
+    down_final,
+    mask_final,
+    layer_ref,
+    delta_ref,
+    key_sum,
+    value_sum,
+    query_turned,
+    delta_turned,
+    dmask_sum,
+    part,
+    twin,
+    first,
+    second,
+    third,
+    mask_part,
+    mask_first,
+    mask_second,
+    mask_third,
+    layer_tree,
+    layer_own,
+    *sems,
+):
+    net = Net(*sems)
+    x, c, leaf = net.x, net.c, net.leaf
+    trunk = TRUNK * block
+    wide = 3 * block
+    low = low_lanes()
+    rows_all, width_all = query_ref.shape
+    pairs = width_all // (2 * LOW_HALF)
+    half = rows_all // 2
+    piece = width_all
+    total = 8 * pairs
+    ready = 2 * (pairs - 1)
+    chunks = []
+
+    def dense(load, twin_load, final):
+        k = len(chunks)
+        chunks.append(
+            Scatter(
+                net,
+                k,
+                load,
+                part.at[k],
+                twin.at[k],
+                twin_load,
+                first.at[k],
+                second.at[k],
+                third.at[k],
+                final,
+            )
+        )
+
+    def own(core):
+        return pl.ds(pl.multiple_of(core * piece, piece), piece)
+
+    dense(
+        out_grad.at[:, :, :, :, own(c)],
+        out_grad.at[:, :, :, :, own(1 - c)],
+        lambda a, b: out_final.at[a, :, own(b)],
+    )
+    for j in range(4):
+        dense(
+            down_grad.at[:, :, j, :, :, own(c)],
+            down_grad.at[:, :, j, :, :, own(1 - c)],
+            lambda a, b, j=j: down_final.at[j, a, :, own(b)],
+        )
+    for j in range(4):
+        dense(
+            up_grad.at[:, :, :, :, own(4 * c + j)],
+            up_grad.at[:, :, :, :, own(4 * (1 - c) + j)],
+            lambda a, b, j=j: up_final.at[a, :, own(4 * b + j)],
+        )
+    dense_count = len(chunks)
+    for h in range(ready):
+        chunks.append(
+            Scatter(
+                net,
+                len(chunks),
+                None,
+                mask_part.at[h],
+                None,
+                None,
+                mask_first.at[h],
+                mask_second.at[h],
+                mask_third.at[h],
+                lambda a, b, h=h: mask_final.at[b, h, a],
+            )
+        )
+    spare = len(chunks)
+    net.greet(("x", "c", "xc", "y", 1, 2, 3))
+
+    mine = pl.ds(pl.multiple_of(c * half, half), half)
+    delta_cross = net.remote(spare, 0, delta_half.at[:, own(1 - c)], delta_ref.at[mine], "c")
+    delta_cross.start()
+    delta_home = net.stay(spare, delta_half.at[:, own(c)], delta_ref.at[mine])
+    delta_home.start()
+
+    layer_rows = layer_ref.shape[1]
+    per = layer_rows // block
+    blocks_mine = pl.ds(c * 2 * per, 2 * per)
+
+    class Output:
+        def copies(self):
+            return (
+                net.remote(spare, 1, layer_half, layer_tree.at[blocks_mine], "c"),
+                net.remote(spare, 2, layer_own.at[1 - x], layer_ref.at[x], "x"),
+            )
+
+        def home(self):
+            return net.stay(spare + 1, layer_half, layer_tree.at[blocks_mine])
+
+        def step(self, number):
+            to_core, to_chip = self.copies()
+            if number == 0:
+                to_core.start()
+                self.home().start()
+            elif number == 1:
+                to_core.wait_recv()
+                self.home().wait()
+                for a in range(2):
+                    for b in range(per):
+                        place = place_ref[(2 * a + c) * per + b]
+                        layer_own[a, b * block : (b + 1) * block] = layer_tree[place]
+                to_chip.start()
+                layer_ref[x] = layer_own[x]
+            elif number == 2:
+                to_chip.wait_recv()
+
+        def finish(self):
+            for copy in self.copies():
+                copy.wait_send()
+
+    output = Output()
+    plan = []
+    pace, lag0, lag1, lag2, lag3, lag4 = BACK_PLAN
+    for i, chunk in enumerate(chunks):
+        start = i * pace
+        if i >= dense_count:
+            start = max(start, 8.0 * ((i - dense_count) // 2 + 1) + 0.1 * (i % 2))
+        for step in range(6):
+            plan.append((start, chunk, step))
+            start = start + (lag0, lag1, lag2, lag3, lag4, 0)[step]
+    plan += [(0.0, output, 0), (1.0, output, 1), (12.0, output, 2)]
+    plan = sorted(plan, key=lambda entry: entry[0])
+    delta_home.wait()
+    delta_cross.wait_recv()
+
+    def one_pair(p, carry):
+        pair_lanes = pl.ds(pl.multiple_of(p * 2 * LOW_HALF, 2 * LOW_HALF), 2 * LOW_HALF)
+        key_sum[...] = jnp.zeros_like(key_sum)
+        value_sum[...] = jnp.zeros_like(value_sum)
+        dmask_sum[...] = jnp.zeros_like(dmask_sum)
+        query_turned[...] = query_ref[:, pair_lanes].astype(F32).T.astype(BF)
+        delta_turned[...] = delta_ref[:, pair_lanes].astype(F32).T.astype(BF)
+
+        def work(rows, mask_place, columns):
+            query = query_ref[rows, pair_lanes]
+            delta = delta_ref[rows, pair_lanes]
+            product = delta.astype(F32) * out_ref[rows, pair_lanes].astype(F32)
+            logs = log_ref[rows, pair_lanes]
+            dqueries = []
+            for which in range(2):
+                start = LOW_HALF * which
+                lanes = slice(start, start + LOW_HALF)
+                query_head = one_head(query, which)
+                delta_head = one_head(delta, which)
+                log = logs[:, start : start + 1]
+                row_term = jnp.sum(product[:, lanes], axis=1, keepdims=True)
+                mask_rows = mask_ref[2 * p + which, mask_place, :]
+                dquery = 0.0
+                for place, tiles in columns:
+                    key = key_ref[place, pair_lanes]
+                    value = value_ref[place, pair_lanes]
+                    probs = jnp.exp(dot_nt(query_head, key) - log)
+                    pair = dot_nt(delta_head, value) * probs
+                    mask = mask_rows if tiles is None else mask_columns(mask_rows, tiles, block)
+                    mask = mask.astype(F32)
+                    if tiles is None:
+                        dmask_sum[which, mask_place, :] += pair
+                    else:
+                        for tile in sorted(set(tiles)):
+                            dmask_sum[which, mask_place, tile * block : (tile + 1) * block] += sum(
+                                pair[:, a * block : (a + 1) * block]
+                                for a, t in enumerate(tiles)
+                                if t == tile
+                            )
+                    dscores = (pair * mask - probs * row_term).astype(BF)
+                    weights = (probs * mask).astype(BF)
+                    dquery = dquery + dot_nn(dscores, key)
+                    key_sum[lanes, place] += dot_nn(query_turned[lanes, rows], dscores)
+                    value_sum[lanes, place] += dot_nn(delta_turned[lanes, rows], weights)
+                dqueries.append(dquery)
+            both = jnp.where(low, dqueries[0], dqueries[1]) * scale
+            dquery_ref[rows, pair_lanes] = both.astype(BF)
+
+        def trunk_rows(index, carry):
+            run_plan(plan, 8 * p + index, total)
+            rows = pl.ds(pl.multiple_of(index * block, block), block)
+            columns = [(pl.ds(0, trunk), None)]
+            columns += [(pl.ds(trunk + wide * g, wide), (1, 0, 1)) for g in range(GROUPS)]
+            work(rows, rows, columns)
+            return carry
+
+        lax.fori_loop(0, TRUNK, trunk_rows, 0)
+
+        def group_rows(group, carry):
+            run_plan(plan, 8 * p + 4 + group, total)
+            base = pl.multiple_of(trunk + wide * group, block)
+            for row in range(3):
+                rows = pl.ds(pl.multiple_of(base + block * row, block), block)
+                tile = 0 if row == 1 else 1
+                start, width, tiles = group_columns(row, block)
+                near = pl.ds(pl.multiple_of(base + start, block), width)
+                work(rows, pl.ds(tile * block, block), [(pl.ds(0, trunk), None), (near, tiles)])
+            return carry
+
+        lax.fori_loop(0, GROUPS, group_rows, 0)
+        dkey_ref[:, pair_lanes] = key_sum[...].T.astype(BF)
+        dvalue_ref[:, pair_lanes] = value_sum[...].T.astype(BF)
+        shape = mask_part.shape[2:]
+
+        def put(target, at):
+            for which in range(2):
+                for tile in range(LINE):
+                    strip = dmask_sum[which, tile * block : (tile + 1) * block, :].astype(BF)
+                    target[at + which, tile] = strip.reshape(shape)
+
+        @pl.when(p < pairs - 1)
+        def _():
+            put(mask_part, 2 * p)
+
+        @pl.when(p == pairs - 1)
+        def _():
+            put(last_ref, 0)
+
+        return carry
+
+    lax.fori_loop(0, pairs, one_pair, 0)
+    run_rest(plan, total)
+    for chunk in chunks + [output]:
+        chunk.finish()
+    delta_cross.wait_send()
+
+
+def scatter_buffers(count, shape, with_twin):
+    half, columns = shape
+    whole = pltpu.VMEM((count, LINE, 2, 2, half, columns), BF)
+    line = pltpu.VMEM((count, LINE, half, columns), BF)
+    return (
+        [whole]
+        + ([whole] if with_twin else [])
+        + [
+            line,
+            pltpu.VMEM((count, 2, LINE, half, columns), BF),
+            pltpu.VMEM((count, LINE - 1, half, columns), BF),
+        ]
+    )
+
+
+def attend_back_wide(
+    query, key, value, mask, out, logs, delta, layer, place, out_grad, up_grad, down_grad, block, scale
+):
+    rows, width = query.shape
+    heads, span, _ = mask.shape
+    half = rows // 2
+    strip = span // 16
+    own_rows = rows // 4
+    piece_rows = out_grad.shape[3]
+    like = jax.ShapeDtypeStruct
+    return pl.pallas_call(
+        functools.partial(attend_back_wide_kernel, block, scale),
+        name="attend_back_wide",
+        in_specs=[VMEM] * 6 + [ANY] * 2 + [SMEM] + [ANY] * 3,
+        out_specs=[VMEM] * 9,
+        out_shape=[like((rows, width), BF)] * 3
+        + [
+            like((2, LINE, 2, 2, strip, span), BF),
+            like((2,) + out_grad.shape[3:], BF),
+            like((2,) + up_grad.shape[3:], BF),
+            like((4, 2) + down_grad.shape[4:], BF),
+            like((2, heads - 2, 2, strip, span), BF),
+            like((2, own_rows, 2 * width), BF),
+        ],
+        scratch_shapes=[
+            pltpu.VMEM((rows, width), BF),
+            pltpu.VMEM((2 * LOW_HALF, rows), F32),
+            pltpu.VMEM((2 * LOW_HALF, rows), F32),
+            pltpu.VMEM((2 * LOW_HALF, rows), BF),
+            pltpu.VMEM((2 * LOW_HALF, rows), BF),
+            pltpu.VMEM((2, span, span), F32),
+        ]
+        + scatter_buffers(9, (piece_rows, width), True)
+        + scatter_buffers(heads - 2, (strip, span), False)
+        + [
+            pltpu.VMEM((2 * layer.shape[0],) + layer.shape[1:], BF),
+            pltpu.VMEM((2, own_rows, 2 * width), BF),
+        ]
+        + copy_semaphores(15, 11),
+        compiler_params=pltpu.CompilerParams(
+            collective_id=2, has_side_effects=True, vmem_limit_bytes=VMEM_LIMIT
+        ),
+    )(query, key, value, mask, out, logs, delta, layer, place, out_grad, up_grad, down_grad)
+
+
+def leave_kernel(
+    block,
+    tokens_ref,
+    place_ref,
+    last_ref,
+    joined_ref,
+    vectors_ref,
+    mask_final,
+    joined_final,
+    tokens_out,
+    vectors_out,
+    part,
+    first,
+    second,
+    third,
+    mask_part,
+    mask_first,
+    mask_second,
+    mask_third,
+    give,
+    keep,
+    got,
+    sums,
+    from_core,
+    from_chip,
+    from_y,
+    from_z,
+    *sems,
+):
+    net = Net(*sems)
+    x, c, y, z = net.x, net.c, net.y, net.z
+    width = joined_ref.shape[4] // 3
+    chunks = []
+    for h in range(2):
+        chunks.append(
+            Scatter(
+                net,
+                len(chunks),
+                last_ref.at[h],
+                mask_part.at[h],
+                None,
+                None,
+                mask_first.at[h],
+                mask_second.at[h],
+                mask_third.at[h],
+                lambda a, b, h=h: mask_final.at[b, h, a],
+            )
+        )
+
+    def joined_place(a, b, i):
+        return joined_final.at[a, :, pl.ds(pl.multiple_of((2 * i + b) * width, width), width)]
+
+    for i in range(3):
+        chunks.append(
+            Scatter(
+                net,
+                len(chunks),
+                joined_ref.at[:, :, :, :, pl.ds(i * width, width)],
+                part.at[i],
+                None,
+                None,
+                first.at[i],
+                second.at[i],
+                third.at[i],
+                lambda a, b, i=i: joined_place(a, b, i),
+            )
+        )
+    row = len(chunks)
+    net.greet(("x", "c", "xc", "y", 1, 2, 3))
+    for chunk in chunks:
+        chunk.step(0)
+    own_rows = give.shape[1]
+    per = own_rows // block
+
+    def collect(target, core):
+        for a in range(2):
+            for b in range(per):
+                place = place_ref[(2 * a + core) * per + b]
+                target[a, b * block : (b + 1) * block] = tokens_ref[place]
+
+    collect(give, 1 - c)
+    core_copy = net.remote(row, 0, give, got, "c")
+    core_copy.start()
+    vector_copies = (
+        net.remote(row, 1, vectors_ref, from_core, "c"),
+        net.remote(row, 2, sums.at[0], from_chip, "x"),
+        net.remote(row, 3, sums.at[1, :, 1 - y], from_y, "y"),
+    )
+    vector_copies[0].start()
+    for chunk in chunks:
+        chunk.step(1)
+    collect(keep, c)
+    core_copy.wait_recv()
+    keep[...] = (keep[...].astype(F32) + got[...].astype(F32)).astype(BF)
+    chip_copy = net.remote(row, 4, keep.at[1 - x], tokens_out.at[x], "x")
+    chip_copy.start()
+    tokens_out[x] = keep[x]
+    vector_copies[0].wait_recv()
+    sums[0] = vectors_ref[...] + from_core[...]
+    vector_copies[1].start()
+    for chunk in chunks:
+        chunk.step(2)
+    vector_copies[1].wait_recv()
+    sums[1] = sums[0] + from_chip[...]
+    vector_copies[2].start()
+    for chunk in chunks:
+        chunk.step(3)
+    vector_copies[2].wait_recv()
+    sums[2, :, 0] = sums[1, :, y] + from_y[...]
+    line_copies = [
+        net.remote(row, 4 + step, sums.at[2, (z + step) % LINE, 0], from_z.at[step - 1], step)
+        for step in (1, 2, 3)
+    ]
+    for copy in line_copies:
+        copy.start()
+    for chunk in chunks:
+        chunk.step(4)
+    total = sums[2, z, 0]
+    for i, copy in enumerate(line_copies):
+        copy.wait_recv()
+        total = total + from_z[i]
+    vectors_out[...] = total
+    for chunk in chunks:
+        chunk.step(5)
+    chip_copy.wait_recv()
+    for chunk in chunks:
+        chunk.finish()
+    core_copy.wait_send()
+    chip_copy.wait_send()
+    for copy in vector_copies + tuple(line_copies):
+        copy.wait_send()
+
+
+def leave(tokens, place, last, joined, vectors, block):
+    blocks, _, width = tokens.shape
+    like = jax.ShapeDtypeStruct
+    own_rows = blocks * block // 4
+    strip, span = last.shape[4:]
+    half, columns = joined.shape[3:]
+    return pl.pallas_call(
+        functools.partial(leave_kernel, block),
+        name="leave",
+        in_specs=[VMEM, SMEM, ANY, ANY, VMEM],
+        out_specs=[VMEM] * 4,
+        out_shape=[
+            like((2, 2, 2, strip, span), BF),
+            like((2, half, 2 * columns), BF),
+            like((2, own_rows, width), BF),
+            like(vectors.shape[2:], F32),
+        ],
+        scratch_shapes=scatter_buffers(3, (half, columns // 3), False)
+        + scatter_buffers(2, (strip, span), False)
+        + [pltpu.VMEM((2, own_rows, width), BF)] * 3
+        + [
+            pltpu.VMEM((3,) + vectors.shape, F32),
+            pltpu.VMEM(vectors.shape, F32),
+            pltpu.VMEM(vectors.shape, F32),
+            pltpu.VMEM(vectors.shape[:1] + vectors.shape[2:], F32),
+            pltpu.VMEM((LINE - 1,) + vectors.shape[2:], F32),
+        ]
+        + copy_semaphores(6, 11),
+        compiler_params=pltpu.CompilerParams(
+            collective_id=3, has_side_effects=True, vmem_limit_bytes=VMEM_LIMIT
+        ),
+    )(tokens, place, last, joined, vectors)
+
+
 def gather_rows(array, axis=0):
     return lax.all_gather(array, "fsdp", axis=axis, tiled=True)
 
@@ -550,6 +1701,219 @@
     )
 
 
+def fast_device(
+    layer_entry_matrix,
+    loss_sensitivity,
+    ancestor_block_table,
+    gate_trained_scores,
+    gate_random_jitter,
+    softening_scale,
+    triple_projection_matrix,
+    asker_constant_vector,
+    content_constant_vector,
+    mixer_exit_matrix,
+    mixer_exit_constant,
+    mixer_scaling_factor,
+    mixer_recentering_term,
+    dense_expand_matrix,
+    dense_expand_constant,
+    dense_contract_matrix,
+    dense_contract_constant,
+    dense_scaling_factor,
+    dense_recentering_term,
+):
+    micro, _, own_rows, width = layer_entry_matrix.shape
+    blocks = ancestor_block_table.shape[2]
+    rows = own_rows * 4
+    block = rows // blocks
+    heads, strip, span = gate_trained_scores.shape
+    leaf = lax.axis_index("leaf")
+    tree, core = leaf // CORES, leaf % CORES
+    mine = width // CORES
+    half = rows // CORES
+    shard = width // 8
+    hidden_shard = dense_contract_matrix.shape[0]
+    score_scale = 1.0 / math.sqrt(width // heads)
+
+    table = lax.dynamic_index_in_dim(ancestor_block_table[:, 0], tree, 0, keepdims=False)
+    order, place = tree_order(table)
+    softened = jax.nn.sigmoid(
+        (gate_trained_scores + gate_random_jitter) / softening_scale[:, None, None]
+    )
+    relaxed = softened.astype(BF).reshape(heads, 2, strip // 2, span)
+    vectors = [
+        asker_constant_vector,
+        content_constant_vector,
+        mixer_exit_constant,
+        mixer_scaling_factor,
+        mixer_recentering_term,
+        dense_contract_constant,
+        dense_scaling_factor,
+        dense_recentering_term,
+        dense_expand_constant,
+    ]
+    sizes = [vector.shape[0] for vector in vectors]
+    used = sum(sizes)
+    flat = jnp.pad(jnp.concatenate(vectors), (0, 2048 - used)).reshape(16, 128)
+
+    tree_tokens, joined_weight, first_masks, packed = enter(
+        layer_entry_matrix[:, 0], triple_projection_matrix.reshape(2, shard // 2, 3 * width), relaxed, flat
+    )
+    packed = packed.reshape(8, 2048).astype(F32)
+    places = [sum(sizes[:i]) for i in range(len(sizes))]
+    (
+        query_bias,
+        value_bias,
+        out_bias,
+        first_gain,
+        first_shift,
+        down_bias,
+        second_gain,
+        second_shift,
+        up_bias,
+    ) = [packed[:, a : a + n].reshape(1, -1) for a, n in zip(places, sizes)]
+
+    def my_part(vector):
+        return lax.dynamic_slice_in_dim(vector, core * mine, mine, 1)
+
+    joined_weight = joined_weight.reshape(width, 3 * mine)
+    tokens, query, key, value = join(
+        order, tree_tokens, joined_weight, my_part(query_bias), my_part(value_bias)
+    )
+    attended_mine, logs, attended, mask, out_weight, up_weight, down_weight, tree_upstream = (
+        attend_wide(
+            query,
+            key,
+            value,
+            first_masks,
+            relaxed,
+            mixer_exit_matrix.reshape(2, shard // 2, width),
+            dense_expand_matrix.reshape(2, shard // 2, -1),
+            dense_contract_matrix.reshape(4, 2, hidden_shard // 8, width),
+            loss_sensitivity[:, 0],
+            block,
+        )
+    )
+    mask = mask.reshape(heads // CORES, span, span)
+    out_weight = out_weight.reshape(width, width)
+    up_weight = up_weight.reshape(width, -1)
+    down_weight = down_weight.reshape(-1, width)
+    half_order = lax.dynamic_slice_in_dim(order, core * (blocks // 2), blocks // 2, 0)
+    upstream = pick(half_order, tree_upstream, block).reshape(half, width).astype(F32)
+    tokens = tokens.reshape(rows, width)
+    rows_mine = lax.dynamic_slice_in_dim(tokens, core * half, half, 0).astype(F32)
+
+    hidden, normed_first, inv_first = layer_norm(
+        rows_mine + dot_nn(attended, out_weight) + out_bias, first_gain, first_shift
+    )
+    hidden_low = hidden.astype(BF)
+    active, slope = gelu_parts(dot_nn(hidden_low, up_weight) + up_bias)
+    active = active.astype(BF)
+    output, normed_second, inv_second = layer_norm(
+        hidden + dot_nn(active, down_weight) + down_bias, second_gain, second_shift
+    )
+    delta_second, second_gain_grad, second_shift_grad = norm_backward(
+        upstream, normed_second, inv_second, second_gain
+    )
+    delta_branch = delta_second.astype(BF)
+    down_weight_grad = dot_tn(active, delta_branch).astype(BF)
+    down_bias_grad = jnp.sum(delta_branch.astype(F32), axis=0)
+    delta_up = (dot_nt(delta_branch, down_weight) * slope).astype(BF)
+    up_weight_grad = dot_tn(hidden_low, delta_up).astype(BF)
+    up_bias_grad = jnp.sum(delta_up.astype(F32), axis=0)
+    delta_first, first_gain_grad, first_shift_grad = norm_backward(
+        delta_second + dot_nt(delta_up, up_weight), normed_first, inv_first, first_gain
+    )
+    delta_proj = delta_first.astype(BF)
+    out_weight_grad = dot_tn(attended, delta_proj).astype(BF)
+    out_bias_grad = jnp.sum(delta_proj.astype(F32), axis=0)
+    delta_attended = dot_nt(delta_proj, out_weight).astype(BF)
+
+    (
+        dquery,
+        dkey,
+        dvalue,
+        last_masks,
+        out_total,
+        up_total,
+        down_total,
+        mask_total,
+        layer_out,
+    ) = attend_back_wide(
+        query,
+        key,
+        value,
+        mask,
+        attended_mine,
+        logs,
+        delta_attended,
+        output.astype(BF).reshape(blocks // 2, block, width),
+        place,
+        out_weight_grad.reshape(LINE, 2, 2, shard // 2, width),
+        up_weight_grad.reshape(LINE, 2, 2, shard // 2, -1),
+        down_weight_grad.reshape(LINE, 2, 4, 2, hidden_shard // 8, width),
+        block,
+        score_scale,
+    )
+    djoined = jnp.concatenate([dquery, dkey, dvalue], axis=1)
+    joined_grad = dot_tn(tokens, djoined).astype(BF)
+    query_bias_grad = jnp.sum(dquery.astype(F32), axis=0)
+    value_bias_grad = jnp.sum(dvalue.astype(F32), axis=0)
+    rest = lax.dynamic_update_slice_in_dim(
+        jnp.zeros((rows, width), F32), delta_first, core * half, 0
+    )
+    dtokens = (dot_nt(djoined, joined_weight) + rest).astype(BF)
+
+    def placed(part):
+        return lax.dynamic_update_slice_in_dim(jnp.zeros((width,), F32), part, core * mine, 0)
+
+    small = (
+        placed(query_bias_grad),
+        placed(value_bias_grad),
+        out_bias_grad,
+        first_gain_grad,
+        first_shift_grad,
+        down_bias_grad,
+        second_gain_grad,
+        second_shift_grad,
+        up_bias_grad,
+    )
+    small = jnp.concatenate([s.reshape(8, -1) for s in small], axis=1)
+    small = jnp.pad(small, ((0, 0), (0, 2048 - used))).reshape(LINE, 2, 16, 128)
+    mask_last, joined_total, tokens_grad, small = leave(
+        dtokens.reshape(blocks, block, width),
+        place,
+        last_masks,
+        joined_grad.reshape(LINE, 2, 2, shard // 2, 3 * mine),
+        small,
+        block,
+    )
+    small = small.reshape(2048)
+    vector_grads = [small[a : a + n] for a, n in zip(places, sizes)]
+    mask_total = jnp.concatenate([mask_total, mask_last], axis=1).reshape(heads, strip, span)
+    mask_gradient = (
+        mask_total.astype(F32) * softened * (1.0 - softened) / softening_scale[:, None, None]
+    )
+    return (
+        layer_out[:, None],
+        tokens_grad[:, None],
+        joined_total.reshape(shard, 3 * width).astype(F32),
+        vector_grads[0],
+        vector_grads[1],
+        out_total.reshape(shard, width).astype(F32),
+        vector_grads[2],
+        vector_grads[3],
+        vector_grads[4],
+        up_total.reshape(shard, -1).astype(F32),
+        vector_grads[8],
+        down_total.reshape(hidden_shard, width).astype(F32),
+        vector_grads[5],
+        vector_grads[6],
+        vector_grads[7],
+        mask_gradient,
+    )
+
+
 def solution(mesh):
     placed = (
         P(None, "fsdp", "leaf", None),
@@ -573,7 +1937,7 @@
         P("fsdp"),
     )
     return jax.shard_map(
-        per_device,
+        fast_device if mesh.shape["fsdp"] == 8 and mesh.shape["leaf"] == 4 else per_device,
         mesh=mesh,
         in_specs=placed,
         out_specs=(

time: 1240 us -> 478 us (0.39)
  waiting for transfers between devices: 754 us -> 0 us
  Pallas kernels: 192 us -> 360 us
  blocking collectives: 75.9 us -> 0 us
  local copies, waits for them, and re-layouts: 64.1 us -> 12 us
  matrix products: 93.7 us -> 73.8 us
  between operations: 15.6 us -> 1.53 us
    reduce_scatter x6 -> x0, waiting for transfers between devices: 377 us -> none  [the longest x5 364 us: owned(): lax.psum_scatter(grad.astype(BF), 'fsdp', scatter_dimension=axis, tiled=T...]
    all_gather x11 -> x0, waiting for transfers between devices: 349 us -> none  [the longest x5 204 us: gather_rows(): return lax.all_gather(array, 'fsdp', axis=axis, tiled=True)]
    pallas_call x8 -> x6, Pallas kernels: 192 us -> 360 us  [the longest x1 134 us: attend_back_wide(): pl.pallas_call(functools.partial(attend_back_wide_kernel, block, scale),...]
    unnamed x1 -> x0, blocking collectives: 37.7 us -> none
    all_gather x1 -> x0, blocking collectives: 32.5 us -> none  [gather_rows(): return lax.all_gather(array, 'fsdp', axis=axis, tiled=True)]
    slice x8 -> x4, local copies, waits for them, and re-layouts: 27.3 us -> 1.26 us  [the longest x2 1.18 us: fast_device(): vector_grads = [small[a:a + n] for a, n in zip(places, sizes)]]
    psum x1 -> x0, waiting for transfers between devices: 24.6 us -> none  [per_device(): lax.psum(matrix, 'leaf').astype(F32)]
    dot_general x4 -> x3, matrix products: 33 us -> 25.9 us  [dot_nn(): return jnp.dot(left, right, preferred_element_type=F32)]
  transfers between devices with their start and end apart: 18 -> 0, of which waited for: 15 -> 0; matrix products, arithmetic and copies ran while one was open for 10% -> 0% of each run, Pallas kernels for 7% -> 0%
where the time goes in v2:
time: 478 us; the launch traced here: 475 us
  Pallas kernels  360 us (75%)
  matrix products  73.8 us (15%)
  other arithmetic  27.3 us (6%)
  local copies, waits for them, and re-layouts  12 us (3%)
    pallas_call x1, Pallas kernels, attend_back_wide(): pl.pallas_call(functools.partial(attend_back_wide_kernel, block, scale),...  134 us
    pallas_call x1, Pallas kernels, attend_wide(): pl.pallas_call(functools.partial(attend_wide_kernel, block), name='attend...  108 us
    pallas_call x1, Pallas kernels, leave(): pl.pallas_call(functools.partial(leave_kernel, block), name='leave', in_s...  55.6 us
    pallas_call x1, Pallas kernels, enter(): pl.pallas_call(enter_kernel, name='enter', in_specs=[ANY] * 4, out_specs=...  48.5 us
    dot_general x3, matrix products, dot_nn(): return jnp.dot(left, right, preferred_element_type=F32)  25.9 us
    dot_general x4, matrix products, dot_nt(): lax.dot_general(left, right, (((1,), (1,)), ((), ())), preferred_element_...  24.8 us
    dot_general x4, matrix products, dot_tn(): lax.dot_general(left, right, (((0,), (0,)), ((), ())), preferred_element_...  23.1 us
    pallas_call x1, Pallas kernels, join(): pl.pallas_call(joined_kernel, name='join', in_specs=[SMEM, ANY, VMEM, VME...  10.9 us

profile of v2, /device:TPU:0, one launch (start us, length us, event | category | flops | bytes accessed | tf_op | source)
XLA Modules:
  0.0 474.9 jit_solution(4390489559576922278)
XLA Ops:
  0.8 3.9 fusion.28
  4.8 0.6 pad_bitcast_fusion.1.vectors_ref
  5.4 48.5 %enter.1 = (bf16[4,512,768]{2,1,0:T(8,128)(2,1)}, bf16[4,2,2,48,1152]{4,3,2,1,0:T(8,128)(2,1)}, bf16[2,4,2,2,32,512]{5,4,3,2,1,0:T(8,128)(2,1)}, bf16[4,2,16,128]{3,2,1,0:T(8,128)(2,1)}) custom-call(bf16[2,512,768]{2,1,0:T(8,128)(2,1)} %bitcast.106, bf16[2,48,2304]{2,1,0:T(8,128)(2,1)} %bitcast.110, bf16[12,2,32,512]{3,2,1,0:T(8,128)(2,1)} %bitcast.93, ...), custom_call_target="tpu_custom_call" | custom-call | tf_op jit(solution)/shard_map/enter/pallas_call | solution.py:626
  53.9 0.8 bitcast_convert_fusion.4
  54.9 0.6 constant_dynamic-slice_fusion
  56.7 0.6 select_reduce_fusion.order_ref
  57.3 10.9 %join.1 = (bf16[16,128,768]{2,1,0:T(8,128)(2,1)}, bf16[2048,384]{1,0:T(8,128)(2,1)}, bf16[2048,384]{1,0:T(8,128)(2,1)}, bf16[2048,384]{1,0:T(8,128)(2,1)}) custom-call(s32[16]{0:T(128)} %select_reduce_fusion.order_ref, bf16[4,512,768]{2,1,0:T(8,128)(2,1)} %get-tuple-element.45.tree_ref, bf16[768,1152]{1,0:T(8,128)(2,1)} %bitcast.101, ...), custom_call_target="tpu_custom_call" | custom-call | tf_op jit(solution)/shard_map/join/pallas_call | solution.py:679
  68.2 108.2 %attend_wide.1 = (bf16[2048,384]{1,0:T(8,128)(2,1)}, f32[2048,384]{1,0:T(8,128)}, bf16[1024,768]{1,0:T(8,128)(2,1)}, bf16[6,4,2,2,32,512]{5,4,3,2,1,0:T(8,128)(2...) custom-call(bf16[2048,384]{1,0:T(8,128)(2,1)} %get-tuple-element.48., ...), custom_call_target="tpu_custom_call" | custom-call | tf_op jit(solution)/shard_map/attend_wide/pallas_call | solution.py:947
  176.6 3.8 fusion.31
  180.4 0.5 multiply_reduce_fusion.3
  181.0 12.7 %multiply_convert_fusion = (bf16[1024,3072]{1,0:T(8,128)(2,1)}, f32[1024,3072]{1,0:T(8,128)}) fusion(f32[3072]{0:T(1024)S(1)} %add.170, bf16[768,3072]{1,0:T(8,128)(2,1)} %bitcast.117, f32[1024,768]{1,0:T(8,128)S(1)} %get-tuple-element.140, f32[768]{0:T(1024)S(1)} %add.167, f32[768]{0:T(1024)S(1)} %mul.275, f32[1024]{0:T(1024)S(1)} %add_rsqrt_fusion.1, ...), kind=kOutput, calls=%fused_computation.8 | convolution fusion | flops 4854644736 | bytes 26765312 | tf_op jit(solution)/shard_map/dot_general | solution.py:45
  193.8 9.5 %fusion.32 = (f32[1024]{0:T(1024)S(1)}, f32[1024,768]{1,0:T(8,128)S(1)}) fusion(f32[768]{0:T(1024)S(1)} %add.176, bf16[1024,3072]{1,0:T(8,128)(2,1)} %get-tuple-element.141, bf16[3072,768]{1,0:T(8,128)(2,1)} %bitcast.121, f32[768]{0:T(1024)S(1)} %add.167, f32[768]{0:T(1024)S(1)} %mul.275, f32[1024]{0:T(1024)S(1)} %add_rsqrt_fusion.1, ...), kind=kOutput, calls=%fused_computation.102 | convolution fusion | flops 4837342208 | bytes 17323008 | tf_op jit(solution)/shard_map/dot_general | solution.py:45
  203.3 0.5 multiply_reduce_fusion.2
  203.9 0.6 dynamic_slice.20.order_ref
  204.5 3.3 pick.1
  208.0 4.0 fusion.12
  212.1 0.7 convert_reduce_fusion.1
  212.8 1.2 convert_reduce_fusion.2
  214.0 7.0 %convolution_convert_fusion = bf16[3072,768]{1,0:T(8,128)(2,1)} fusion(bf16[1024,3072]{1,0:T(8,128)(2,1)S(1)} %bitcast.130, f32[1024,768]{1,0:T(8,128)S(1)} %get-tuple-element.117), kind=kOutput, calls=%fused_computation.10 | convolution fusion | flops 4834983936 | bytes 14155776 | tf_op jit(solution)/shard_map/dot_general | solution.py:53
  221.0 12.0 %convert_reduce_fusion = (f32[3072]{0:T(1024)S(1)}, bf16[1024,3072]{1,0:T(8,128)(2,1)S(1)}) fusion(f32[1024,3072]{1,0:T(8,128)} %get-tuple-element.142, f32[3072]{0:T(1024)S(1)} %add.170, bf16[3072,768]{1,0:T(8,128)(2,1)S(1)} %bitcast.124, f32[1024,768]{1,0:T(8,128)S(1)} %get-tuple-element.117), kind=kOutput, calls=%fused_computation.7 | convolution fusion | flops 4873516032 | bytes 26763264 | tf_op jit(solution)/shard_map/dot_general | solution.py:49
  233.0 8.2 %convolution_convert_fusion.1 = bf16[768,3072]{1,0:T(8,128)(2,1)} fusion(bf16[1024,3072]{1,0:T(8,128)(2,1)S(1)} %get-tuple-element.147, f32[1024,768]{1,0:T(8,128)S(1)} %copy-done.4, f32[768]{0:T(1024)S(1)} %add.167, f32[768]{0:T(1024)S(1)} %mul.275, f32[1024]{0:T(1024)S(1)} %add_rsqrt_fusion.1, f32[1024]{0:T(1024)S(1)} %broadcast_multiply_fusion.4), kind=kOutput, calls=%fused_computation.11 | convolution fusion | flops 4838129664 | bytes 14170112 | tf_op jit(solution)/shard_map/dot_general | solution.py:53
  241.2 5.8 %multiply_reduce_fusion = (f32[768]{0:T(1024)S(1)}, f32[1024]{0:T(1024)S(1)}, f32[1024]{0:T(1024)S(1)}, f32[768]{0:T(1024)S(1)}, f32[1024,768]{1,0:T(8,128)S(1)}) fusion(f32[1024,768]{1,0:T(8,128)S(1)} %copy-done.4, f32[1024]{0:T(1024)S(1)} %add_rsqrt_fusion.1, f32[1024]{0:T(1024)S(1)} %broadcast_multiply_fusion.4, f32[768]{0:T(1024)S(1)} %mul.275, ...), kind=kOutput, calls=%fused_computation.25 | convolution fusion | flops 4839698432 | bytes 20472832 | tf_op jit(solution)/shard_map/dot_general | solution.py:49
  247.0 1.1 convert_reduce_fusion.3
  248.4 2.5 convolution_convert_fusion.4
  250.9 2.7 convolution_convert_fusion.3.delta_half
  253.6 133.7 %attend_back_wide.1 = (bf16[2048,384]{1,0:T(8,128)(2,1)}, bf16[2048,384]{1,0:T(8,128)(2,1)}, bf16[2048,384]{1,0:T(8,128)(2,1)}, bf16[2,4,2,2,32,512]{5,4,3,2,1,0...) custom-call(bf16[2048,384]{1,0:T(8,128)(2,1)} %get-tuple-element.48., ...), custom_call_target="tpu_custom_call" | custom-call | tf_op jit(solution)/shard_map/attend_back_wide/pallas_call | solution.py:1262
  387.4 1.7 convert_reduce_fusion.5
  389.4 1.7 convert_reduce_fusion.4
  392.0 0.6 copy.40
  392.6 1.7 constant_dynamic-update-slice_fusion.2
  394.3 0.3 constant_dynamic-update-slice_fusion.1
  394.7 0.3 constant_dynamic-update-slice_fusion
  395.0 1.3 copy-done.29
  396.3 5.5 %convolution_convert_fusion.2 = bf16[768,1152]{1,0:T(8,128)(2,1)} fusion(bf16[2048,768]{1,0:T(8,128)(2,1)S(1)} %bitcast.126, bf16[2048,1152]{1,0:T(8,128)(2,1)S(1)} %constant_dynamic-update-slice_fusion), kind=kOutput, calls=%fused_computation.12 | convolution fusion | flops 3624763392 | bytes 9633792 | tf_op jit(solution)/shard_map/dot_general | solution.py:53
  401.8 4.3 fusion.33
  406.2 0.7 add_dynamic-update-slice_fusion
  406.9 2.0 convert_element_type.154
  408.9 55.6 %leave.1 = (bf16[2,2,2,32,512]{4,3,2,1,0:T(8,128)(2,1)}, bf16[2,48,2304]{2,1,0:T(8,128)(2,1)}, bf16[2,512,768]{2,1,0:T(8,128)(2,1)}, f32[16,128]{1,0:T(8,128)}) custom-call(bf16[16,128,768]{2,1,0:T(8,128)(2,1)} %bitcast.92, s32[16]{0:T(128)} %copy-done.16, bf16[2,4,2,2,32,512]{5,4,3,2,1,0:T(8,128)(2,1)} %get-tuple-element.65.last_ref, ...), custom_call_target="tpu_custom_call" | custom-call | tf_op jit(solution)/shard_map/leave/pallas_call | solution.py:1436
  464.5 1.1 pad_maximum_fusion
  465.6 1.6 fusion.15
  467.2 1.0 bitcast_convert_fusion.2
  468.2 0.6 fusion.30
  468.8 0.6 slice_bitcast_fusion
  469.4 1.1 bitcast_convert_fusion
  470.5 1.2 bitcast_convert_fusion.1
  471.7 0.7 bitcast_convert_fusion.3
  472.4 1.1 copy.50
  473.6 1.1 copy.51
  (126 shorter events, 3.7 us)
Async XLA Ops:
  0.7 54.8 %copy-start = (s32[2,1,16]{2,1,0:T(1,128)S(1)}, s32[2,1,16]{2,1,0:T(1,128)}, u32[]{:S(2)}) copy-start(s32[2,1,16]{2,1,0:T(1,128)} %param.21) | copy-start | bytes 388
  0.7 4.0 copy-start.20
  0.7 4.0 copy-start.21
  0.7 4.0 copy-start.22
  0.7 4.0 copy-start.23
  0.7 4.0 copy-start.24
  0.7 4.0 copy-start.19
  0.7 4.0 copy-start.25
  0.7 4.0 copy-start.26
  0.7 4.0 copy-start.27
  56.7 119.8 %copy-start.16 = (s32[16]{0:T(128)}, s32[16]{0:T(128)S(1)}, u32[]{:S(2)}) copy-start(s32[16]{0:T(128)S(1)} %fusion.19.place_ref) | copy-start | bytes 196
  180.3 13.4 %copy-start.3 = (f32[1024,768]{1,0:T(8,128)}, f32[1024,768]{1,0:T(8,128)S(1)}, u32[]{:S(2)}) copy-start(f32[1024,768]{1,0:T(8,128)S(1)} %get-tuple-element.140) | copy-start | bytes 9437188
  203.3 0.7 copy-start.28
  208.0 4.0 copy-start.2
  208.0 6.0 %slice-start.4 = ((s8[6291456]{0:T(1024)(128)(4,1)}), s8[4194304]{0:T(1024)(128)(4,1)S(1)}, s32[]{:S(2)}) async-start(s8[6291456]{0:T(1024)(128)(4,1)} %bitcast.129), calls=%async_computation.4 | async-start | bytes 8388608
  212.0 2.0 slice-start.5
  212.8 8.2 %slice-start.2 = ((s8[4718592]{0:T(1024)(128)(4,1)}), s8[4194304]{0:T(1024)(128)(4,1)S(1)}, s32[]{:S(2)}) async-start(s8[4718592]{0:T(1024)(128)(4,1)} %bitcast.122), calls=%async_computation.2 | async-start | bytes 8388608
  214.0 7.0 %slice-start.3 = ((s8[4718592]{0:T(1024)(128)(4,1)}), s8[524288]{0:T(1024)(128)(4,1)S(1)}, s32[]{:S(2)}) async-start(s8[4718592]{0:T(1024)(128)(4,1)} %bitcast.122), calls=%async_computation.3 | async-start | bytes 1048576
  214.0 27.1 %slice-start = ((s8[4718592]{0:T(1024)(128)(4,1)}), s8[4194304]{0:T(1024)(128)(4,1)S(1)}, s32[]{:S(2)}) async-start(s8[4718592]{0:T(1024)(128)(4,1)} %bitcast.118), calls=%async_computation | async-start | bytes 8388608
  221.0 12.0 %copy-start.4 = (f32[1024,768]{1,0:T(8,128)S(1)}, f32[1024,768]{1,0:T(8,128)}, u32[]{:S(2)}) copy-start(f32[1024,768]{1,0:T(8,128)} %copy-done.3) | copy-start | bytes 9437188
  221.0 20.2 %slice-start.1 = ((s8[4718592]{0:T(1024)(128)(4,1)}), s8[524288]{0:T(1024)(128)(4,1)S(1)}, s32[]{:S(2)}) async-start(s8[4718592]{0:T(1024)(128)(4,1)} %bitcast.118), calls=%async_computation.1 | async-start | bytes 1048576
  247.0 1.4 copy-start.30
  248.4 2.5 copy-start.31
  392.0 2.4 copy-start.9
  392.6 2.0 copy-start.5
  394.3 2.0 copy-start.29
  396.3 5.5 %copy-start.7 = (bf16[4,2,2,48,1152]{4,3,2,1,0:T(8,128)(2,1)S(1)}, bf16[4,2,2,48,1152]{4,3,2,1,0:T(8,128)(2,1)}, u32[]{:S(2)}) copy-start(bf16[4,2,2,48,1152]{4,3,2,1,0:T(8,128)(2,1)} %get-tuple-element.46) | copy-start | bytes 5308420
  408.9 55.6 %copy-start.13 = (bf16[2,4,2,32,512]{4,3,2,1,0:T(8,128)(2,1)S(1)}, bf16[2,4,2,32,512]{4,3,2,1,0:T(8,128)(2,1)}, u32[]{:S(2)}) copy-start(bf16[2,4,2,32,512]{4,3,2,1,0:T(8,128)(2,1)} %get-tuple-element.72) | copy-start | bytes 1572868
  408.9 56.7 %copy-start.6 = (f32[12,64,512]{2,1,0:T(8,128)S(1)}, f32[12,64,512]{2,1,0:T(8,128)}, u32[]{:S(2)}) copy-start(f32[12,64,512]{2,1,0:T(8,128)} %get-tuple-element.121) | copy-start | bytes 4718596
  408.9 56.7 %copy-start.18 = (f32[12]{0:T(128)S(1)}, f32[12]{0:T(128)}, u32[]{:S(2)}) copy-start(f32[12]{0:T(128)} %param.24) | copy-start | bytes 148
  464.5 2.7 copy-start.14
  464.5 3.7 copy-start.17
  464.5 4.9 %copy-start.12 = (bf16[4,2,48,768]{3,2,1,0:T(8,128)(2,1)S(1)}, bf16[4,2,48,768]{3,2,1,0:T(8,128)(2,1)}, u32[]{:S(2)}) copy-start(bf16[4,2,48,768]{3,2,1,0:T(8,128)(2,1)} %get-tuple-element.71) | copy-start | bytes 1769476
  465.6 4.9 %copy-start.11 = (bf16[2,48,3072]{2,1,0:T(8,128)(2,1)S(1)}, bf16[2,48,3072]{2,1,0:T(8,128)(2,1)}, u32[]{:S(2)}) copy-start(bf16[2,48,3072]{2,1,0:T(8,128)(2,1)} %get-tuple-element.70) | copy-start | bytes 1769476
  467.2 4.5 copy-start.15
  467.2 5.2 %copy-start.8 = (bf16[2,512,768]{2,1,0:T(8,128)(2,1)S(1)}, bf16[2,512,768]{2,1,0:T(8,128)(2,1)}, u32[]{:S(2)}) copy-start(bf16[2,512,768]{2,1,0:T(8,128)(2,1)} %get-tuple-element.61) | copy-start | bytes 4718596
  469.4 4.2 copy-start.10
  471.7 3.0 copy-start.1
